TPU v7x, 256 devices: a whole 4x4x8 slice. The times are simulated.
256 devices in a mesh: seq: 128 (over z_lo, x, y, core), ch: 2 (over z_hi).
Axes of the slice: x: 4, y: 4, z: 8 (z_hi: 2, z_lo: 4; z = z_hi * 4 + z_lo), core: 2. Of those that a mesh axis runs over, the one named last changes fastest.
Arguments:
- query_branch: bfloat16 [16384, 1024], P('seq', 'ch'), may hold values from -6 to 6
- key_branch: bfloat16 [16384, 1024], P('seq', 'ch'), may hold values from -44.5 to 44.5, as said below
- value_branch: bfloat16 [16384, 1024], P('seq', 'ch'), may hold values from -44.5 to 44.5, as said below
- filter_taps: float32 [16384, 1024], P('seq', 'ch'), may hold values from -1.5 to 1.5, as said below
- skip_gain: float32 [1024], P('ch'), may hold values from -2.8 to 2.8, as said below
- out_weight: bfloat16 [1024, 8192], P('ch'), may hold values from -0.1875 to 0.1875
Outputs:
- mixed: bfloat16 [16384, 8192], P('seq')
Inputs may be any that keep to these rules, and one draw needn't show every extreme that they name: `filter_taps`: real filter taps, one column a channel. `key_branch`: real values. `value_branch`: real values. `skip_gain`: one real number a channel.
All inputs are finite; a program needn't handle non-finite values.
Results may differ from a plain program's by a relative error of at most 0.0049.
Values may be sent and summed in bfloat16 or wider, within the bound.
A program may use at most 128 MiB of HBM per device.

v0:
```python
import math

import jax
import jax.numpy as jnp
from jax import lax
from jax.sharding import PartitionSpec as P

highest = lax.Precision.HIGHEST


def from_partner(shard, axis, apart):
    return lax.ppermute(shard, axis, [(i, i ^ 1 << apart) for i in range(lax.axis_size(axis))])


def complex_mul(signal, twiddle_re, twiddle_im):
    real_part = signal[0] * twiddle_re - signal[1] * twiddle_im
    imag_part = signal[0] * twiddle_im + signal[1] * twiddle_re
    return jnp.stack([real_part, imag_part])


def dft_table(extent, direction):
    counter = jnp.arange(extent, dtype=jnp.int32)
    folded = counter[:, None] * counter[None, :] % extent
    phase_table = direction * 2.0 * math.pi * folded.astype(jnp.float32) / extent
    return (jnp.cos(phase_table), jnp.sin(phase_table))


def apply_table(table, signal, form):
    table_re, table_im = table
    real_part = jnp.einsum(form, table_re, signal[0], precision=highest) - jnp.einsum(
        form, table_im, signal[1], precision=highest
    )
    imag_part = jnp.einsum(form, table_re, signal[1], precision=highest) + jnp.einsum(
        form, table_im, signal[0], precision=highest
    )
    return jnp.stack([real_part, imag_part])


def body(query_branch, key_branch, value_branch, filter_taps, skip_gain, out_weight):
    block_rows, width_dev = key_branch.shape
    devices = lax.axis_size("seq")
    sections = devices.bit_length() - 1
    device_index = lax.axis_index("seq")
    total = block_rows * devices
    product = key_branch.astype(jnp.float32) * value_branch.astype(jnp.float32)
    position = device_index * block_rows + jnp.arange(block_rows, dtype=jnp.int32)
    pad_phase = math.pi * position.astype(jnp.float32) / total
    pad_cos = jnp.cos(pad_phase)[:, None]
    pad_sin = jnp.sin(pad_phase)[:, None]
    zero_block = jnp.zeros_like(product)
    real_stack = jnp.stack([product, product * pad_cos, filter_taps, filter_taps * pad_cos])
    imag_stack = jnp.stack([zero_block, -product * pad_sin, zero_block, -filter_taps * pad_sin])
    signal = jnp.stack([real_stack, imag_stack])
    local_form = "jt,stc->sjc"
    for section in range(sections):
        bit_pos = sections - 1 - section
        half_span = total >> section + 1
        is_lower = device_index // 2**bit_pos % 2 == 0
        turn = -math.pi * (position % half_span).astype(jnp.float32) / half_span
        partner = from_partner(signal, "seq", bit_pos)
        signal = jnp.where(
            is_lower,
            signal + partner,
            complex_mul(partner - signal, jnp.cos(turn)[:, None], jnp.sin(turn)[:, None]),
        )
    spectrum = apply_table(dft_table(block_rows, -1.0), signal, local_form)
    left_spec = spectrum[:, 0:2]
    right_spec = spectrum[:, 2:4]
    joined = jnp.stack(
        [
            left_spec[0] * right_spec[0] - left_spec[1] * right_spec[1],
            left_spec[0] * right_spec[1] + left_spec[1] * right_spec[0],
        ]
    )
    signal = apply_table(dft_table(block_rows, 1.0), joined, local_form)
    for section in reversed(range(sections)):
        bit_pos = sections - 1 - section
        half_span = total >> section + 1
        is_lower = device_index // 2**bit_pos % 2 == 0
        turn = -math.pi * (position % half_span).astype(jnp.float32) / half_span
        twisted = jnp.where(
            is_lower, signal, complex_mul(signal, jnp.cos(turn)[:, None], -jnp.sin(turn)[:, None])
        )
        partner = from_partner(twisted, "seq", bit_pos)
        signal = jnp.where(is_lower, twisted + partner, partner - twisted)
    convolved = (signal[0, 0] + signal[0, 1] * pad_cos - signal[1, 1] * pad_sin) / (2.0 * total)
    gated_values = (
        query_branch.astype(jnp.float32) * (convolved + skip_gain[None, :] * product)
    ).astype(jnp.bfloat16)
    partial_value = jnp.dot(gated_values, out_weight, preferred_element_type=jnp.float32)
    mixed = lax.psum(partial_value, "ch")
    return mixed.astype(jnp.bfloat16)


def solution(mesh):
    return jax.shard_map(
        body,
        mesh=mesh,
        in_specs=(
            P("seq", "ch"),
            P("seq", "ch"),
            P("seq", "ch"),
            P("seq", "ch"),
            P("ch"),
            P("ch", None),
        ),
        out_specs=P("seq", None),
        check_vma=False,
    )
```

profile of v0, /device:TPU:1, one launch (start us, length us, event | category | flops | bytes accessed | tf_op | source)
XLA Modules:
  0.0 759.6 jit_solution(2688769268955418462)
XLA Ops:
  4.9 3.8 collective-permute-start
  8.8 89.9 %collective-permute-done = f32[2,4,128,512]{2,3,1,0:T(8,128)} collective-permute-done((f32[2,4,128,512]{2,3,1,0:T(8,128)}, f32[2,4,128,512]{2,3,1,0:T(8,128)}, u32[]{:S(2)}, u32[]{:S(2)}) %collective-permute-start) | collective-permute-done | bytes 2097184 | tf_op jit(solution)/shard_map/ppermute | solution.py:12
  100.7 3.6 maximum_select_fusion
  106.2 44.8 %collective-permute-done.1 = f32[2,4,128,512]{2,3,1,0:T(8,128)} collective-permute-done((f32[2,4,128,512]{2,3,1,0:T(8,128)}, f32[2,4,128,512]{2,3,1,0:T(8,128)}, u32[]{:S(2)}, u32[]{:S(2)}) %collective-permute-start.1) | collective-permute-done | bytes 2097184 | tf_op jit(solution)/shard_map/ppermute | solution.py:12
  151.0 2.9 fusion.117
  155.2 4.2 maximum_select_fusion.1
  159.4 3.0 collective-permute-start.2
  162.4 43.8 %collective-permute-done.2 = f32[2,4,128,512]{2,3,1,0:T(8,128)S(1)} collective-permute-done((f32[2,4,128,512]{2,3,1,0:T(8,128)}, f32[2,4,128,512]{2,3,1,0:T(8,128)S(1)}, u32[]{:S(2)}, u32[]{:S(2)}) %collective-permute-start.2) | collective-permute-done | bytes 2097184 | tf_op jit(solution)/shard_map/ppermute | solution.py:12
  206.1 2.6 sub.155
  213.7 42.8 %collective-permute-done.3 = f32[2,4,128,512]{2,3,1,0:T(8,128)} collective-permute-done((f32[2,4,128,512]{2,3,1,0:T(8,128)S(1)}, f32[2,4,128,512]{2,3,1,0:T(8,128)}, u32[]{:S(2)}, u32[]{:S(2)}) %collective-permute-start.3) | collective-permute-done | bytes 2097184 | tf_op jit(solution)/shard_map/ppermute | solution.py:12
  258.6 3.2 maximum_select_fusion.3
  261.8 3.0 collective-permute-start.4
  264.8 41.9 %collective-permute-done.4 = f32[2,4,128,512]{2,3,1,0:T(8,128)S(1)} collective-permute-done((f32[2,4,128,512]{2,3,1,0:T(8,128)}, f32[2,4,128,512]{2,3,1,0:T(8,128)S(1)}, u32[]{:S(2)}, u32[]{:S(2)}) %collective-permute-start.4) | collective-permute-done | bytes 2097184 | tf_op jit(solution)/shard_map/ppermute | solution.py:12
  306.7 2.6 sub.159
  314.2 41.1 %collective-permute-done.5 = f32[2,4,128,512]{2,3,1,0:T(8,128)} collective-permute-done((f32[2,4,128,512]{2,3,1,0:T(8,128)S(1)}, f32[2,4,128,512]{2,3,1,0:T(8,128)}, u32[]{:S(2)}, u32[]{:S(2)}) %collective-permute-start.5) | collective-permute-done | bytes 2097184 | tf_op jit(solution)/shard_map/ppermute | solution.py:12
  357.3 3.2 maximum_select_fusion.5
  360.5 5.8 collective-permute-start.6
  366.4 3.9 collective-permute-done.6
  372.3 1.9 maximum_select_fusion.6
  383.3 2.2 collective-permute-done.7
  387.4 23.0 %collective-permute-done.8 = f32[2,2,128,512]{2,3,1,0:T(8,128)S(1)} collective-permute-done((f32[2,2,128,512]{2,3,1,0:T(8,128)S(1)}, f32[2,2,128,512]{2,3,1,0:T(8,128)S(1)}, u32[]{:S(2)}, u32[]{:S(2)}) %collective-permute-start.8) | collective-permute-done | bytes 1048608 | tf_op jit(solution)/shard_map/ppermute | solution.py:12
  410.8 3.2 collective-permute-start.9
  414.0 22.0 %collective-permute-done.9 = f32[2,2,128,512]{2,3,1,0:T(8,128)S(1)} collective-permute-done((f32[2,2,128,512]{2,3,1,0:T(8,128)S(1)}, f32[2,2,128,512]{2,3,1,0:T(8,128)S(1)}, u32[]{:S(2)}, u32[]{:S(2)}) %collective-permute-start.9) | collective-permute-done | bytes 1048608 | tf_op jit(solution)/shard_map/ppermute | solution.py:12
  437.8 21.3 %collective-permute-done.10 = f32[2,2,128,512]{2,3,1,0:T(8,128)S(1)} collective-permute-done((f32[2,2,128,512]{2,3,1,0:T(8,128)S(1)}, f32[2,2,128,512]{2,3,1,0:T(8,128)S(1)}, u32[]{:S(2)}, u32[]{:S(2)}) %collective-permute-start.10) | collective-permute-done | bytes 1048608 | tf_op jit(solution)/shard_map/ppermute | solution.py:12
  459.4 2.8 collective-permute-start.11
  462.3 20.6 %collective-permute-done.11 = f32[2,2,128,512]{2,3,1,0:T(8,128)S(1)} collective-permute-done((f32[2,2,128,512]{2,3,1,0:T(8,128)S(1)}, f32[2,2,128,512]{2,3,1,0:T(8,128)S(1)}, u32[]{:S(2)}, u32[]{:S(2)}) %collective-permute-start.11) | collective-permute-done | bytes 1048608 | tf_op jit(solution)/shard_map/ppermute | solution.py:12
  483.3 4.5 collective-permute-start.12
  487.9 19.6 %collective-permute-done.12 = f32[2,2,128,512]{2,3,1,0:T(8,128)S(1)} collective-permute-done((f32[2,2,128,512]{2,3,1,0:T(8,128)S(1)}, f32[2,2,128,512]{2,3,1,0:T(8,128)S(1)}, u32[]{:S(2)}, u32[]{:S(2)}) %collective-permute-start.12) | collective-permute-done | bytes 1048608 | tf_op jit(solution)/shard_map/ppermute | solution.py:12
  508.8 4.1 collective-permute-start.13
  514.0 43.9 %collective-permute-done.13 = f32[2,2,128,512]{2,3,1,0:T(8,128)S(1)} collective-permute-done((f32[2,2,128,512]{2,3,1,0:T(8,128)}, f32[2,2,128,512]{2,3,1,0:T(8,128)S(1)}, u32[]{:S(2)}, u32[]{:S(2)}) %collective-permute-start.13) | collective-permute-done | bytes 1048608 | tf_op jit(solution)/shard_map/ppermute | solution.py:12
  558.1 6.8 fusion.23
  564.9 194.7 %all-reduce.1 = bf16[128,8192]{1,0:T(8,128)(2,1)} all-reduce(f32[128,8192]{1,0:T(8,128)} %fusion.23), channel_id=1, replica_groups=mesh['seq'=128,'ch'=2] {'ch'}, use_global_device_ids=true, to_apply=%region_0.1 | all-reduce | flops 1048576 | bytes 6291456 | tf_op jit(solution)/shard_map/psum | solution.py:91
  (87 shorter events, 42.5 us)
Async XLA Ops:
  4.9 93.7 %collective-permute-start = (f32[2,4,128,512]{2,3,1,0:T(8,128)}, f32[2,4,128,512]{2,3,1,0:T(8,128)}, u32[]{:S(2)}, u32[]{:S(2)}) collective-permute-start(f32[2,4,128,512]{2,3,1,0:T(8,128)} %pad_maximum_fusion), channel_id=1, source_target_pairs={{0,128},{2,130},{4,132},{6,134},{8,136},{10,138},{12,140},{14,142}... | collective-permute-start | bytes 6291464 | tf_op jit(solution)/shard_map/ppermute | solution.py:12
  100.7 3.6 copy-start
  104.3 46.7 %collective-permute-start.1 = (f32[2,4,128,512]{2,3,1,0:T(8,128)}, f32[2,4,128,512]{2,3,1,0:T(8,128)}, u32[]{:S(2)}, u32[]{:S(2)}) collective-permute-start(f32[2,4,128,512]{2,3,1,0:T(8,128)} %maximum_select_fusion), channel_id=1, source_target_pairs={{0,64},{2,66},{4,68},{6,70},{8,72},{10,74},{12,76},{14,78},{16,80}... | collective-permute-start | bytes 6291464 | tf_op jit(solution)/shard_map/ppermute | solution.py:12
  154.0 1.2 copy-start.1
  159.4 46.8 %collective-permute-start.2 = (f32[2,4,128,512]{2,3,1,0:T(8,128)}, f32[2,4,128,512]{2,3,1,0:T(8,128)S(1)}, u32[]{:S(2)}, u32[]{:S(2)}) collective-permute-start(f32[2,4,128,512]{2,3,1,0:T(8,128)} %maximum_select_fusion.1), channel_id=1, source_target_pairs={{0,32},{2,34},{4,36},{6,38},{8,40},{10,42},{12,44},{14,46},{16,48}... | collective-permute-start | bytes 6291464 | tf_op jit(solution)/shard_map/ppermute | solution.py:12
  206.1 2.6 copy-start.2
  208.7 1.6 copy-start.3
  212.2 44.3 %collective-permute-start.3 = (f32[2,4,128,512]{2,3,1,0:T(8,128)S(1)}, f32[2,4,128,512]{2,3,1,0:T(8,128)}, u32[]{:S(2)}, u32[]{:S(2)}) collective-permute-start(f32[2,4,128,512]{2,3,1,0:T(8,128)S(1)} %maximum_select_fusion.2), channel_id=1, source_target_pairs={{0,16},{2,18},{4,20},{6,22},{8,24},{10,26},{12,28},{14,30},{16,0},... | collective-permute-start | bytes 6291464 | tf_op jit(solution)/shard_map/ppermute | solution.py:12
  261.8 44.9 %collective-permute-start.4 = (f32[2,4,128,512]{2,3,1,0:T(8,128)}, f32[2,4,128,512]{2,3,1,0:T(8,128)S(1)}, u32[]{:S(2)}, u32[]{:S(2)}) collective-permute-start(f32[2,4,128,512]{2,3,1,0:T(8,128)} %maximum_select_fusion.3), channel_id=1, source_target_pairs={{0,8},{2,10},{4,12},{6,14},{8,0},{10,2},{12,4},{14,6},{16,24},{18,... | collective-permute-start | bytes 6291464 | tf_op jit(solution)/shard_map/ppermute | solution.py:12
  306.7 2.6 copy-start.4
  309.3 1.6 copy-start.5
  312.8 42.5 %collective-permute-start.5 = (f32[2,4,128,512]{2,3,1,0:T(8,128)S(1)}, f32[2,4,128,512]{2,3,1,0:T(8,128)}, u32[]{:S(2)}, u32[]{:S(2)}) collective-permute-start(f32[2,4,128,512]{2,3,1,0:T(8,128)S(1)} %maximum_select_fusion.4), channel_id=1, source_target_pairs={{0,4},{2,6},{4,0},{6,2},{8,12},{10,14},{12,8},{14,10},{16,20},{18,... | collective-permute-start | bytes 6291464 | tf_op jit(solution)/shard_map/ppermute | solution.py:12
  360.5 9.8 %collective-permute-start.6 = (f32[2,4,128,512]{2,3,1,0:T(8,128)}, f32[2,4,128,512]{2,3,1,0:T(8,128)S(1)}, u32[]{:S(2)}, u32[]{:S(2)}) collective-permute-start(f32[2,4,128,512]{2,3,1,0:T(8,128)} %maximum_select_fusion.5), channel_id=1, source_target_pairs={{0,2},{2,0},{4,6},{6,4},{8,10},{10,8},{12,14},{14,12},{16,18},{18,... | collective-permute-start | bytes 6291464 | tf_op jit(solution)/shard_map/ppermute | solution.py:12
  382.8 2.7 collective-permute-start.7
  385.9 24.5 %collective-permute-start.8 = (f32[2,2,128,512]{2,3,1,0:T(8,128)S(1)}, f32[2,2,128,512]{2,3,1,0:T(8,128)S(1)}, u32[]{:S(2)}, u32[]{:S(2)}) collective-permute-start(f32[2,2,128,512]{2,3,1,0:T(8,128)S(1)} %maximum_select_fusion.8), channel_id=1, source_target_pairs={{0,4},{2,6},{4,0},{6,2},{8,12},{10,14},{12,8},{14,10},{16,20},{18,... | collective-permute-start | bytes 3145736 | tf_op jit(solution)/shard_map/ppermute | solution.py:12
  410.8 25.3 %collective-permute-start.9 = (f32[2,2,128,512]{2,3,1,0:T(8,128)S(1)}, f32[2,2,128,512]{2,3,1,0:T(8,128)S(1)}, u32[]{:S(2)}, u32[]{:S(2)}) collective-permute-start(f32[2,2,128,512]{2,3,1,0:T(8,128)S(1)} %maximum_select_fusion.9), channel_id=1, source_target_pairs={{0,8},{2,10},{4,12},{6,14},{8,0},{10,2},{12,4},{14,6},{16,24},{18,... | collective-permute-start | bytes 3145736 | tf_op jit(solution)/shard_map/ppermute | solution.py:12
  436.4 22.6 %collective-permute-start.10 = (f32[2,2,128,512]{2,3,1,0:T(8,128)S(1)}, f32[2,2,128,512]{2,3,1,0:T(8,128)S(1)}, u32[]{:S(2)}, u32[]{:S(2)}) collective-permute-start(f32[2,2,128,512]{2,3,1,0:T(8,128)S(1)} %maximum_select_fusion.10), channel_id=1, source_target_pairs={{0,16},{2,18},{4,20},{6,22},{8,24},{10,26},{12,28},{14,30},{16,0},... | collective-permute-start | bytes 3145736 | tf_op jit(solution)/shard_map/ppermute | solution.py:12
  459.4 23.5 %collective-permute-start.11 = (f32[2,2,128,512]{2,3,1,0:T(8,128)S(1)}, f32[2,2,128,512]{2,3,1,0:T(8,128)S(1)}, u32[]{:S(2)}, u32[]{:S(2)}) collective-permute-start(f32[2,2,128,512]{2,3,1,0:T(8,128)S(1)} %maximum_select_fusion.11), channel_id=1, source_target_pairs={{0,32},{2,34},{4,36},{6,38},{8,40},{10,42},{12,44},{14,46},{16,48}... | collective-permute-start | bytes 3145736 | tf_op jit(solution)/shard_map/ppermute | solution.py:12
  483.3 24.2 %collective-permute-start.12 = (f32[2,2,128,512]{2,3,1,0:T(8,128)S(1)}, f32[2,2,128,512]{2,3,1,0:T(8,128)S(1)}, u32[]{:S(2)}, u32[]{:S(2)}) collective-permute-start(f32[2,2,128,512]{2,3,1,0:T(8,128)S(1)} %maximum_select_fusion.12), channel_id=1, source_target_pairs={{0,64},{2,66},{4,68},{6,70},{8,72},{10,74},{12,76},{14,78},{16,80}... | collective-permute-start | bytes 3145736 | tf_op jit(solution)/shard_map/ppermute | solution.py:12
  508.8 49.1 %collective-permute-start.13 = (f32[2,2,128,512]{2,3,1,0:T(8,128)}, f32[2,2,128,512]{2,3,1,0:T(8,128)S(1)}, u32[]{:S(2)}, u32[]{:S(2)}) collective-permute-start(f32[2,2,128,512]{2,3,1,0:T(8,128)} %maximum_select_fusion.13), channel_id=1, source_target_pairs={{0,128},{2,130},{4,132},{6,134},{8,136},{10,138},{12,140},{14,142}... | collective-permute-start | bytes 3145736 | tf_op jit(solution)/shard_map/ppermute | solution.py:12
  514.0 44.1 %copy-start.6 = (f32[512]{0:T(512)S(1)}, f32[512]{0:T(512)}, u32[]{:S(2)}) copy-start(f32[512]{0:T(512)} %param.10) | copy-start | bytes 6148
where the time goes:
time: 762 us; the launch traced here: 760 us
  waiting for transfers between devices  461 us (60%)
  blocking collectives  195 us (26%)
  other arithmetic  42.9 us (6%)
  starting transfers between devices  37.9 us (5%)
  matrix products  15 us (2%)
  local copies, waits for them, and re-layouts  7.85 us (1%)
    ppermute x14, waiting for transfers between devices, from_partner(): lax.ppermute(shard, axis, [(i, i ^ 1 << apart) for i in range(lax.axis_si...  461 us
    psum x1, blocking collectives, body(): mixed = lax.psum(partial_value, 'ch')  195 us
    ppermute x14, starting transfers between devices, from_partner(): lax.ppermute(shard, axis, [(i, i ^ 1 << apart) for i in range(lax.axis_si...  37.9 us
    select_n x7, other arithmetic, body(): jnp.where(is_lower, signal + partner, complex_mul(partner - signal, jnp.c...  19.9 us
    sub x7, other arithmetic, body(): partner - signal  15.3 us
  transfers between devices with their start and end apart: 14, of which 14 were waited for; matrix products, arithmetic and copies ran while one was open for 0% of the time, Pallas kernels for 0%

commit v1 on v0

v1 whole, which is shorter than its diff:
```python
import math

import jax
import jax.numpy as jnp
import numpy as np
from jax import lax
from jax.sharding import PartitionSpec as P

bf16 = jnp.bfloat16
f32 = jnp.float32


def tables(blocks, span):
    alpha = np.arange(blocks)[:, None] + 0.5
    fine = np.arange(span)
    ahead = 2.0 * np.pi * alpha * np.arange(blocks)[None, :] / (2 * blocks)
    turn = 2.0 * np.pi * alpha * fine[None, :] / (2 * blocks * span)
    inner = 2.0 * np.pi * (fine[:, None] * fine[None, :] % span) / span
    first = np.concatenate([np.cos(ahead), -np.sin(ahead)], 0)
    second = np.block([[np.cos(inner), -np.sin(inner)], [np.sin(inner), np.cos(inner)]])
    back = np.block([[np.cos(inner), np.sin(inner)], [-np.sin(inner), np.cos(inner)]])
    last = np.concatenate([np.cos(ahead), -np.sin(ahead)], 0).T / (blocks * span)
    as32 = lambda t: jnp.asarray(t.astype(np.float32))
    return as32(first), as32(np.cos(turn)), as32(-np.sin(turn)), as32(second), as32(back), as32(last)


def mm(form, a, b):
    return jnp.einsum(form, a, b, precision=lax.Precision.HIGH, preferred_element_type=f32)


def body(query_branch, key_branch, value_branch, filter_taps, skip_gain, out_weight):
    span, width = key_branch.shape
    n_seq = lax.axis_size("seq")
    n_ch = lax.axis_size("ch")
    me = lax.axis_index("seq")
    rows = width // n_seq
    mine = lax.dynamic_slice_in_dim(out_weight, me * rows, rows, 0)
    theirs = lax.ppermute(mine, "ch", [(i, i ^ 1) for i in range(n_ch)])
    other_weight = lax.all_gather(theirs, "seq", tiled=True)

    product = key_branch.astype(f32) * value_branch.astype(f32)
    pair = jnp.stack([product.T, filter_taps.T]).astype(bf16)
    pair = pair.reshape(2, n_seq, rows, span).transpose(1, 0, 2, 3)
    got = lax.all_to_all(pair, "seq", 0, 0)
    first, tw_re, tw_im, second, back, last = tables(n_seq, span)
    x = mm("ka,ascb->sckb", first.astype(f32), got.astype(f32))
    re, im = x[:, :, :n_seq], x[:, :, n_seq:]
    x = jnp.concatenate([re * tw_re - im * tw_im, re * tw_im + im * tw_re], -1)
    x = mm("sckb,bj->sckj", x, second)
    re, im = x[..., :span], x[..., span:]
    z = jnp.concatenate([re[0] * re[1] - im[0] * im[1], re[0] * im[1] + im[0] * re[1]], -1)
    z = mm("ckj,jb->ckb", z, back)
    re, im = z[..., :span], z[..., span:]
    z = jnp.concatenate([re * tw_re + im * tw_im, im * tw_re - re * tw_im], 1)
    y = mm("ak,ckb->acb", last, z)
    conv = lax.all_to_all(y.astype(bf16), "seq", 0, 0)
    convolved = conv.reshape(width, span).T.astype(f32)
    gated = (query_branch.astype(f32) * (convolved + skip_gain[None, :] * product)).astype(bf16)
    gated_other = lax.ppermute(gated, "ch", [(i, i ^ 1) for i in range(n_ch)])
    mixed = jnp.dot(gated, out_weight, preferred_element_type=f32)
    mixed = mixed + jnp.dot(gated_other, other_weight, preferred_element_type=f32)
    return mixed.astype(bf16)


def solution(mesh):
    return jax.shard_map(
        body,
        mesh=mesh,
        in_specs=(P("seq", "ch"), P("seq", "ch"), P("seq", "ch"), P("seq", "ch"), P("ch"), P("ch", None)),
        out_specs=P("seq", None),
        check_vma=False,
    )
```

time: 762 us -> 258 us (0.34)
  waiting for transfers between devices: 461 us -> 162 us
  blocking collectives: 195 us -> 24.9 us
  other arithmetic: 42.9 us -> 1.49 us
  starting transfers between devices: 37.9 us -> 19.1 us
  between operations: 0.43 us -> 13.6 us
  local copies, waits for them, and re-layouts: 7.85 us -> 18.3 us
    ppermute x14 -> x2, waiting for transfers between devices: 461 us -> 1.76 us  [the longest x1 1.75 us: body(): theirs = lax.ppermute(mine, 'ch', [(i, i ^ 1) for i in range(n_ch)])]
    psum x1 -> x0, blocking collectives: 195 us -> none  [body(): mixed = lax.psum(partial_value, 'ch')]
    all_gather x0 -> x1, waiting for transfers between devices: none -> 149 us  [body(): other_weight = lax.all_gather(theirs, 'seq', tiled=True)]
    ppermute x14 -> x2, starting transfers between devices: 37.9 us -> 12.6 us  [the longest x1 7.83 us: body(): theirs = lax.ppermute(mine, 'ch', [(i, i ^ 1) for i in range(n_ch)])]
    all_to_all x0 -> x1, blocking collectives: none -> 24.9 us  [body(): got = lax.all_to_all(pair, 'seq', 0, 0)]
    select_n x21 -> x0, other arithmetic: 22.6 us -> none  [the longest x7 19.9 us: body(): jnp.where(is_lower, signal + partner, complex_mul(partner - signal, jnp.c...]
    sub x21 -> x2, other arithmetic: 17.7 us -> 1.07 us  [the longest x1 1.01 us: body(): x = jnp.concatenate([re * tw_re - im * tw_im, re * tw_im + im * tw_re], -1)]
    all_to_all x0 -> x1, waiting for transfers between devices: none -> 10.9 us  [body(): conv = lax.all_to_all(y.astype(bf16), 'seq', 0, 0)]
  transfers between devices with their start and end apart: 14 -> 4, of which waited for: 14 -> 3; matrix products, arithmetic and copies ran while one was open for 0% -> 11% of each run, Pallas kernels for 0% -> 0%
where the time goes in v1:
time: 258 us
  waiting for transfers between devices  162 us (63%)
  blocking collectives  24.9 us (10%)
  starting transfers between devices  19.1 us (7%)
  matrix products  18.4 us (7%)
  local copies, waits for them, and re-layouts  18.3 us (7%)
  between operations  13.6 us (5%)
    all_gather x1, waiting for transfers between devices, body(): other_weight = lax.all_gather(theirs, 'seq', tiled=True)  149 us
    all_to_all x1, blocking collectives, body(): got = lax.all_to_all(pair, 'seq', 0, 0)  24.9 us
    unnamed x19, local copies, waits for them, and re-layouts  16.4 us
    all_to_all x1, waiting for transfers between devices, body(): conv = lax.all_to_all(y.astype(bf16), 'seq', 0, 0)  10.9 us
    ppermute x1, starting transfers between devices, body(): theirs = lax.ppermute(mine, 'ch', [(i, i ^ 1) for i in range(n_ch)])  7.83 us
    dot_general x1, matrix products, body(): jnp.dot(gated_other, other_weight, preferred_element_type=f32)  7.3 us
    dot_general x1, matrix products, body(): mixed = jnp.dot(gated, out_weight, preferred_element_type=f32)  6.71 us
    all_to_all x1, starting transfers between devices, body(): conv = lax.all_to_all(y.astype(bf16), 'seq', 0, 0)  6.44 us
  transfers between devices with their start and end apart: 4, of which 3 were waited for; matrix products, arithmetic and copies ran while one was open for 11% of the time, Pallas kernels for 0%

profile of v1, /device:TPU:1, one launch (start us, length us, event | category | flops | bytes accessed | tf_op | source)
XLA Modules:
  0.0 257.7 jit_solution(10220324187690331667)
XLA Ops:
  6.5 0.0 copy-start.6
  6.6 0.0 all-gather.3.cloned.1.call-start
  6.6 1.0 constant_dynamic-slice_fusion
  7.6 7.8 %collective-permute-start.1 = (bf16[4,8192]{1,0:T(4,128)(2,1)S(1)}, bf16[4,8192]{1,0:T(4,128)(2,1)S(1)}, u32[]{:S(2)}, u32[]{:S(2)}) collective-permute-start(bf16[4,8192]{1,0:T(4,128)(2,1)S(1)} %constant_dynamic-slice_fusion), channel_id=1, source_target_pairs={{0,1},{1,0},{2,3},{3,2},{4,5},{5,4},{6,7},{7,6},{8,9},{9,8},{10,11... | collective-permute-start | bytes 196616 | tf_op jit(solution)/shard_map/ppermute | solution.py:38
  15.4 1.8 collective-permute-done.1
  17.2 0.6 copy-done.5
  17.8 0.0 all-gather.3.cloned.1.call-update
  17.8 1.0 copy.29
  18.9 1.0 copy.30
  19.9 1.1 copy.31
  21.0 0.2 maximum_bitcast_fusion
  21.2 0.1 copy.32
  21.3 24.9 %all_to_all.10 = bf16[128,2,4,128]{3,2,1,0:T(4,128)(2,1)S(1)} all-to-all(bf16[128,2,4,128]{3,2,1,0:T(4,128)(2,1)S(1)} %copy.32), channel_id=1, replica_groups=mesh['seq'=128,'ch'=2] {'seq'}, dimensions={0} | all-to-all | bytes 524288 | tf_op jit(solution)/shard_map/all_to_all | solution.py:44
  46.2 1.4 convolution_bitcast_fusion
  47.6 1.0 multiply_subtract_fusion
  48.6 2.0 fusion.2
  50.6 0.1 subtract_bitcast_fusion
  50.7 0.4 fusion.6
  51.1 0.0 copy-done.3
  51.1 0.1 multiply_add_fusion.1
  51.2 0.6 fusion.1
  51.8 0.8 copy.38
  52.6 6.4 %all-to-all-start.1 = ((bf16[128,4,128]{2,1,0:T(4,128)(2,1)}), bf16[128,4,128]{2,1,0:T(4,128)(2,1)S(1)}, u32[]{:S(2)}, u32[]{:S(2)}) async-start(bf16[128,4,128]{2,1,0:T(4,128)(2,1)} %copy.38), calls=%async_computation.1 | async-start | bytes 262144 | tf_op jit(solution)/shard_map/all_to_all | solution.py:56
  59.0 0.1 copy.28
  59.2 10.9 %all-to-all-done.1 = bf16[128,4,128]{2,1,0:T(4,128)(2,1)S(1)} async-done(((bf16[128,4,128]{2,1,0:T(4,128)(2,1)}), bf16[128,4,128]{2,1,0:T(4,128)(2,1)S(1)}, u32[]{:S(2)}, u32[]{:S(2)}) %all-to-all-start.1) | async-done | bytes 131104 | tf_op jit(solution)/shard_map/all_to_all | solution.py:56
  70.1 0.1 fusion.15
  70.2 4.8 %collective-permute-start = (bf16[128,512]{0,1:T(8,128)(2,1)S(1)}, bf16[128,512]{0,1:T(8,128)(2,1)S(1)}, u32[]{:S(2)}, u32[]{:S(2)}) collective-permute-start(bf16[128,512]{0,1:T(8,128)(2,1)S(1)} %fusion.15), channel_id=1, source_target_pairs={{0,1},{1,0},{2,3},{3,2},{4,5},{5,4},{6,7},{7,6},{8,9},{9,8},{10,11... | collective-permute-start | bytes 393224 | tf_op jit(solution)/shard_map/ppermute | solution.py:59
  75.0 6.7 %fusion.21 = f32[128,8192]{1,0:T(8,128)} fusion(bf16[128,512]{0,1:T(8,128)(2,1)S(1)} %fusion.15, bf16[512,8192]{1,0:T(8,128)(2,1)} %param.17), kind=kOutput, calls=%fused_computation.34 | convolution fusion | flops 1073741824 | bytes 12713984 | tf_op jit(solution)/shard_map/dot_general | solution.py:60
  81.7 149.3 %all-gather.3.cloned.1.call-done = bf16[128,4,8192]{2,1,0:T(4,128)(2,1)} async-done(((bf16[1,4,8192]{2,1,0:T(4,128)(2,1)}), bf16[128,4,8192]{2,1,0:T(4,128)(2,1)}) %all-gather.3.cloned.1.call-update) | async-done | bytes 8388624 | tf_op jit(solution)/shard_map/all_gather | solution.py:39
  231.0 12.5 %reshape.23 = bf16[512,8192]{1,0:T(8,128)(2,1)} reshape(bf16[128,4,8192]{2,1,0:T(4,128)(2,1)} %all-gather.3.cloned.1.call-done) | data formatting | bytes 16777216
  243.6 0.0 collective-permute-done
  243.6 7.3 %fusion = bf16[128,8192]{1,0:T(8,128)(2,1)} fusion(f32[128,8192]{1,0:T(8,128)} %fusion.21, bf16[128,512]{0,1:T(8,128)(2,1)S(1)} %collective-permute-done, bf16[512,8192]{1,0:T(8,128)(2,1)} %reshape.23), kind=kOutput, calls=%fused_computation.1 | convolution fusion | flops 1075838976 | bytes 14811136 | tf_op jit(solution)/shard_map/dot_general | solution.py:61
  (12 shorter events, 0.1 us)
Async XLA Ops:
  6.5 44.1 %copy-start = (f32[256,256,1]{1,0,2:T(8,128)S(1)}, f32[256,256,1]{1,0,2:T(8,128)}, u32[]{:S(2)}) copy-start(f32[256,256,1]{1,0,2:T(8,128)} %constant.32) | copy-start | bytes 786436
  6.5 44.5 %copy-start.3 = (f32[128,128]{1,0:T(8,128)S(1)}, f32[128,128]{1,0:T(8,128)}, u32[]{:S(2)}) copy-start(f32[128,128]{1,0:T(8,128)} %constant.34) | copy-start | bytes 196612
  6.5 44.6 %copy-start.4 = (f32[128,128]{1,0:T(8,128)S(1)}, f32[128,128]{1,0:T(8,128)}, u32[]{:S(2)}) copy-start(f32[128,128]{1,0:T(8,128)} %constant.33) | copy-start | bytes 196612
  6.5 44.6 %copy-start.2 = (f32[128,256,1]{1,0,2:T(8,128)S(1)}, f32[128,256,1]{1,0,2:T(8,128)}, u32[]{:S(2)}) copy-start(f32[128,256,1]{1,0,2:T(8,128)} %constant.35) | copy-start | bytes 393220
  6.5 52.5 %copy-start.1 = (bf16[128,512]{1,0:T(8,128)(2,1)S(1)}, bf16[128,512]{1,0:T(8,128)(2,1)}, u32[]{:S(2)}) copy-start(bf16[128,512]{1,0:T(8,128)(2,1)} %param.12) | copy-start | bytes 393220
  6.5 63.5 %copy-start.6 = (f32[512]{0:T(512)S(1)}, f32[512]{0:T(512)}, u32[]{:S(2)}) copy-start(f32[512]{0:T(512)} %param.16) | copy-start | bytes 6148
  6.6 224.5 %all-gather.3.cloned.1.call-start = ((), (), s32[]{:S(2)}) async-start(), calls=%async_computation.2 | async-start | bytes 8454144 | tf_op jit(solution)/shard_map/all_gather | solution.py:39
  7.6 9.6 %collective-permute-start.1 = (bf16[4,8192]{1,0:T(4,128)(2,1)S(1)}, bf16[4,8192]{1,0:T(4,128)(2,1)S(1)}, u32[]{:S(2)}, u32[]{:S(2)}) collective-permute-start(bf16[4,8192]{1,0:T(4,128)(2,1)S(1)} %constant_dynamic-slice_fusion), channel_id=1, source_target_pairs={{0,1},{1,0},{2,3},{3,2},{4,5},{5,4},{6,7},{7,6},{8,9},{9,8},{10,11... | collective-permute-start | bytes 196616 | tf_op jit(solution)/shard_map/ppermute | solution.py:38
  17.2 0.6 copy-start.5
  52.6 17.5 %all-to-all-start.1 = ((bf16[128,4,128]{2,1,0:T(4,128)(2,1)}), bf16[128,4,128]{2,1,0:T(4,128)(2,1)S(1)}, u32[]{:S(2)}, u32[]{:S(2)}) async-start(bf16[128,4,128]{2,1,0:T(4,128)(2,1)} %copy.38), calls=%async_computation.1 | async-start | bytes 262144 | tf_op jit(solution)/shard_map/all_to_all | solution.py:56
  70.2 173.3 %collective-permute-start = (bf16[128,512]{0,1:T(8,128)(2,1)S(1)}, bf16[128,512]{0,1:T(8,128)(2,1)S(1)}, u32[]{:S(2)}, u32[]{:S(2)}) collective-permute-start(bf16[128,512]{0,1:T(8,128)(2,1)S(1)} %fusion.15), channel_id=1, source_target_pairs={{0,1},{1,0},{2,3},{3,2},{4,5},{5,4},{6,7},{7,6},{8,9},{9,8},{10,11... | collective-permute-start | bytes 393224 | tf_op jit(solution)/shard_map/ppermute | solution.py:59
Sparse Core Ops, SparseCore 0:
  18.0 213.0 all-gather.2

commit v2 on v1

v2 whole, which is shorter than its diff:
```python
import functools
import math

import jax
import jax.numpy as jnp
import numpy as np
from jax import lax
from jax.experimental import pallas as pl
from jax.experimental.pallas import tpu as pltpu
from jax.sharding import PartitionSpec as P

bf16 = jnp.bfloat16
f32 = jnp.float32
MESH = pl.DeviceIdType.MESH
SPAN = 128
BLOCKS = 128
CH = 4
TILE = 512
QUARTER = 2048


def split(t):
    hi = t.astype(bf16)
    return hi, (t - hi.astype(f32)).astype(bf16)


def tables():
    n = 2 * BLOCKS
    at = np.arange(BLOCKS)
    a = (at % 8) // 2 * 32 + at // 8 * 2 + at % 2
    alpha = np.arange(BLOCKS)[:, None] + 0.5
    fine = np.arange(SPAN)
    ahead = 2.0 * np.pi * alpha * a[None, :] / n
    turn = 2.0 * np.pi * alpha * fine[None, :] / (n * SPAN)
    inner = 2.0 * np.pi * (fine[:, None] * fine[None, :] % SPAN) / SPAN
    first = np.concatenate([np.cos(ahead), -np.sin(ahead)], 0)
    second = np.block([[np.cos(inner), -np.sin(inner)], [np.sin(inner), np.cos(inner)]])
    back = np.block([[np.cos(inner), np.sin(inner)], [-np.sin(inner), np.cos(inner)]])
    last = first.T / (BLOCKS * SPAN)

    def parts(t):
        hi = t.astype(jnp.bfloat16)
        return hi, (t - hi.astype(np.float64)).astype(jnp.bfloat16)

    fh, fl = parts(first)
    sh, sl = parts(second)
    bh, bl = parts(back)
    lh, ll = parts(last)
    return (
        jnp.asarray(np.concatenate([fh, fl], 1)),
        jnp.asarray(np.concatenate([sh, sh, sl], 0)),
        jnp.asarray(np.concatenate([bh, bh, bl], 0)),
        jnp.asarray(np.concatenate([lh, lh, ll], 1)),
        jnp.asarray(np.stack([np.cos(turn), -np.sin(turn)]).astype(np.float32)),
    )


def kernel(
    q_ref, k_ref, v_ref, taps_ref, skip_ref, t1_ref, t2_ref, t3_ref, t4_ref, tw_ref, w_ref, out_ref,
    s1, r1, r2, s1q, r1q, r2q, s3, r3, r4, wown, wo, acc, rows8, rows4, xcat, lhs2, lhs3, rhs4,
    own_sem, p1_s, p1_r, p1q_s, p1q_r, p2_s, p2_r, p2q_s, p2q_r, p3_s, p3_r, p4_s, p4_r,
    seed_s, seed_r, st1_s, st1_r, st2_s, st2_r, d2d_s, d2d_r,
):
    me = lax.axis_index("seq")
    g = lax.axis_index("ch")
    z, xy, k = me // 32, me // 2 % 16, me % 2
    x, y = xy // 4, xy % 4
    zk = z * 2 + k

    def dev(z_, xy_, k_, g_):
        return (z_ * 32 + xy_ * 2 + k_, g_)

    def remote(src, dst, ss, rs, to):
        return pltpu.make_async_remote_copy(
            src_ref=src, dst_ref=dst, send_sem=ss, recv_sem=rs, device_id=to, device_id_type=MESH
        )

    barrier = pltpu.get_barrier_semaphore()

    @pl.loop(1, 16)
    def _(i):
        pl.semaphore_signal(barrier, inc=1, device_id=dev(z, (xy + i) % 16, k, g), device_id_type=MESH)

    @pl.loop(1, 8)
    def _(i):
        to = (zk + i) % 8
        pl.semaphore_signal(barrier, inc=1, device_id=dev(to // 2, xy, to % 2, g), device_id_type=MESH)

    @pl.loop(0, 8)
    def _(i):
        pl.semaphore_signal(barrier, inc=1, device_id=dev(i // 2, xy, i % 2, 1 - g), device_id_type=MESH)

    own = pltpu.make_async_copy(w_ref, wown, own_sem)
    own.start()

    ut = (k_ref[...].astype(f32) * v_ref[...].astype(f32)).T
    ht = taps_ref[...].T
    both = jnp.concatenate([ut.reshape(BLOCKS, CH, SPAN), ht.reshape(BLOCKS, CH, SPAN)], 1).astype(bf16)
    both = both.reshape(4, 16, 2, 2 * CH, SPAN)
    for i in range(8):
        s1[i] = both[i // 2, :, i % 2]

    pl.semaphore_wait(barrier, 30)

    def p1(i, src, dst, ss, rs):
        to = (zk + i) % 8
        return remote(src.at[to], dst.at[zk], ss.at[to], rs.at[zk], dev(to // 2, xy, to % 2, g))

    def p1_from(i, src, dst, ss, rs):
        fr = (zk + 8 - i) % 8
        return remote(src.at[fr], dst.at[fr], ss.at[fr], rs.at[fr], dev(fr // 2, xy, fr % 2, g))

    def p2(i, src, dst, ss, rs):
        to = (xy + i) % 16
        return remote(src.at[:, to], dst.at[xy], ss.at[to], rs.at[xy], dev(z, to, k, g))

    def p2_from(i, src, dst, ss, rs):
        fr = (xy + 16 - i) % 16
        return remote(src.at[:, fr], dst.at[fr], ss.at[fr], rs.at[fr], dev(z, fr, k, g))

    def p3(i):
        to = (xy + i) % 16
        return remote(s3.at[to], r3.at[xy], p3_s.at[to], p3_r.at[xy], dev(z, to, k, g))

    def p3_from(i):
        fr = (xy + 16 - i) % 16
        return remote(s3.at[fr], r3.at[fr], p3_s.at[fr], p3_r.at[fr], dev(z, fr, k, g))

    def p4(i, group):
        to = (zk + i) % 8
        return remote(
            r3.at[:, to], r4.at[g, z, :, k], p4_s.at[group, to], p4_r.at[g, zk], dev(to // 2, xy, to % 2, group)
        )

    def p4_from(i, group):
        fr = (zk + 8 - i) % 8
        return remote(
            r3.at[:, fr], r4.at[group, fr // 2, :, fr % 2], p4_s.at[group, fr], p4_r.at[group, fr],
            dev(fr // 2, xy, fr % 2, group),
        )

    def uv(h):
        return (x, y) if h == 0 else (y, x)

    def place(h, u, v):
        return u % 4 * 4 + v % 4 if h == 0 else v % 4 * 4 + u % 4

    def block(h, sub, at):
        return wo.at[h, sub, k * 16 + at]

    def seed(h, sub, from_own):
        zn = (g * 4 + z + 7 + 2 * h) % 8
        src = w_ref.at[
            pl.ds(pl.multiple_of((k * 16 + xy) * 16, 16), 16), pl.ds(pl.multiple_of((h * 2 + sub) * QUARTER, QUARTER), QUARTER)
        ] if from_own else block(h, sub, xy)
        return remote(src, block(h, sub, xy), seed_s.at[h, sub], seed_r.at[h, sub], dev(zn % 4, xy, k, zn // 4))

    def st1(h, side, sub, off=0):
        u, v = uv(h)
        at = place(h, u + off + 4, v)
        slot = 0 if off == 0 else 1
        to = place(h, u + (1 if side == 0 else 3), v)
        return remote(
            block(h, sub, at), block(h, sub, at), st1_s.at[h, slot, side, sub], st1_r.at[h, slot, side, sub], dev(z, to, k, g)
        )

    def st2(h, e, side, sub, off=0):
        u, v = uv(h)
        at = place(h, u + e + 4, v + off + 4)
        slot = 0 if off == 0 else 1
        to = place(h, u, v + (1 if side == 0 else 3))
        return remote(
            block(h, sub, at), block(h, sub, at), st2_s.at[h, e % 4, slot, side, sub], st2_r.at[h, e % 4, slot, side, sub],
            dev(z, to, k, g),
        )

    def d2d(h, at, core):
        return remote(
            wo.at[h, :, core * 16 + at], wo.at[h, :, core * 16 + at], d2d_s.at[h, at], d2d_r.at[h, at], dev(z, xy, 1 - k, g)
        )

    def spread(h, e, sub):
        for side in (0, 1):
            st2(h, e, side, sub).start()

    def seed_step_of(h, sub):
        seed(h, sub, False).wait_recv()

        @pl.when(z != 3 * h)
        def _():
            seed(h, sub, False).start()

        for side in (0, 1):
            st1(h, side, sub).start()
        spread(h, 0, sub)
        if sub == 1:
            d2d(h, xy, k).start()

    def seed_steps(first):
        for h in (0, 1):

            @pl.when((z >= 2) == ((h == 0) == first))
            def _():
                for sub in (0, 1):
                    seed_step_of(h, sub)

    def ring1(h):
        u, v = uv(h)
        for sub in (0, 1):
            st1(h, 0, sub).wait_recv()
            if sub == 0:
                st1(h, 0, 0, -1).start()
            st1(h, 1, sub).wait_recv()
            if sub == 1:
                st1(h, 1, 1, 1).start()
            spread(h, -1, sub)
            spread(h, 1, sub)
        d2d(h, place(h, u + 3, v), k).start()
        d2d(h, place(h, u + 1, v), k).start()

    def ring1_far(h):
        u, v = uv(h)
        st1(h, 0, 0, -1).wait_recv()
        spread(h, 2, 0)
        st1(h, 1, 1, 1).wait_recv()
        spread(h, 2, 1)
        d2d(h, place(h, u + 2, v), k).start()

    def ring2(h, e):
        u, v = uv(h)
        for sub in (0, 1):
            st2(h, e, 0, sub).wait_recv()
            if sub == 0:
                st2(h, e, 0, 0, -1).start()
            st2(h, e, 1, sub).wait_recv()
            if sub == 1:
                st2(h, e, 1, 1, 1).start()
        d2d(h, place(h, u + e + 4, v + 3), k).start()
        d2d(h, place(h, u + e + 4, v + 1), k).start()

    def ring2_far(h, e):
        u, v = uv(h)
        st2(h, e, 0, 0, -1).wait_recv()
        st2(h, e, 1, 1, 1).wait_recv()
        d2d(h, place(h, u + e + 4, v + 2), k).start()

    @pl.loop(1, 8)
    def _(i):
        p1(i, s1, r1, p1_s, p1_r).start()

    for h in (0, 1):

        @pl.when(z == 3 * h)
        def _():
            for sub in (0, 1):
                seed(h, sub, True).start()

    qt = q_ref[...].astype(f32).T.reshape(BLOCKS, CH, SPAN).astype(bf16).reshape(4, 16, 2, CH, SPAN)
    for i in range(8):
        s1q[i] = qt[i // 2, :, i % 2]

    @pl.loop(1, 8)
    def _(i):
        p1(i, s1q, r1q, p1q_s, p1q_r).start()

    r1[zk] = s1[zk]
    r1q[zk] = s1q[zk]

    seed_steps(True)

    @pl.loop(1, 8)
    def _(i):
        p1_from(i, s1, r1, p1_s, p1_r).wait_recv()

    @pl.loop(1, 16)
    def _(i):
        p2(i, r1, r2, p2_s, p2_r).start()

    r2[xy] = r1[:, xy]

    @pl.loop(1, 8)
    def _(i):
        p1_from(i, s1q, r1q, p1q_s, p1q_r).wait_recv()

    @pl.loop(1, 16)
    def _(i):
        p2(i, r1q, r2q, p2q_s, p2q_r).start()

    r2q[xy] = r1q[:, xy]

    seed_steps(False)

    @pl.loop(1, 16)
    def _(i):
        p2_from(i, r1, r2, p2_s, p2_r).wait_recv()

    rows8[...] = r2[...].reshape(BLOCKS, 2 * CH, SPAN).astype(f32).reshape(BLOCKS * 2 * CH, SPAN)
    for r in range(2 * CH):
        part = rows8[pl.ds(r, BLOCKS, stride=2 * CH), :].astype(bf16)
        xcat[0:BLOCKS, r * SPAN : (r + 1) * SPAN] = part
        xcat[BLOCKS : 2 * BLOCKS, r * SPAN : (r + 1) * SPAN] = part
    for r in range(2 * CH):
        got = jnp.dot(t1_ref[...], xcat[:, r * SPAN : (r + 1) * SPAN], preferred_element_type=f32)
        re, im = got[:BLOCKS], got[BLOCKS:]
        hi, lo = split(jnp.concatenate([re * tw_ref[0] - im * tw_ref[1], re * tw_ref[1] + im * tw_ref[0]], 1))
        lhs2[r * BLOCKS : (r + 1) * BLOCKS, 0:256] = hi
        lhs2[r * BLOCKS : (r + 1) * BLOCKS, 256:512] = lo
        lhs2[r * BLOCKS : (r + 1) * BLOCKS, 512:768] = hi

    ring1(0)
    ring1(1)

    for c in range(CH):
        rows = pl.ds(c * BLOCKS, BLOCKS)
        left = jnp.dot(lhs2[rows, :], t2_ref[...], preferred_element_type=f32)
        right = jnp.dot(lhs2[pl.ds((c + CH) * BLOCKS, BLOCKS), :], t2_ref[...], preferred_element_type=f32)
        lr, li, rr, ri = left[:, :SPAN], left[:, SPAN:], right[:, :SPAN], right[:, SPAN:]
        hi, lo = split(jnp.concatenate([lr * rr - li * ri, lr * ri + li * rr], 1))
        lhs3[rows, 0:256] = hi
        lhs3[rows, 256:512] = lo
        lhs3[rows, 512:768] = hi

    ring1_far(0)
    ring1_far(1)

    for c in range(CH):
        rows = pl.ds(c * BLOCKS, BLOCKS)
        got = jnp.dot(lhs3[rows, :], t3_ref[...], preferred_element_type=f32)
        re, im = got[:, :SPAN], got[:, SPAN:]
        cols = pl.ds(c * SPAN, SPAN)
        hi, lo = split(jnp.concatenate([re * tw_ref[0] + im * tw_ref[1], im * tw_ref[0] - re * tw_ref[1]], 0))
        rhs4[0:256, cols] = hi
        rhs4[256:512, cols] = lo
        rhs4[512:768, cols] = hi

    @pl.loop(1, 16)
    def _(i):
        p2_from(i, r1q, r2q, p2q_s, p2q_r).wait_recv()

    rows4[...] = r2q[...].reshape(BLOCKS, CH, SPAN).astype(f32).reshape(BLOCKS * CH, SPAN)
    for c in range(CH):
        conv = jnp.dot(t4_ref[...], rhs4[:, c * SPAN : (c + 1) * SPAN], preferred_element_type=f32)
        at = pl.ds(c, BLOCKS, stride=CH)
        signal = rows8[pl.ds(c, BLOCKS, stride=2 * CH), :]
        rows4[at, :] = rows4[at, :] * (conv + skip_ref[0, me * CH + c] * signal)
    s3[...] = rows4[...].astype(bf16).reshape(16, 8, CH, SPAN)

    @pl.loop(1, 16)
    def _(i):
        p3(i).start()

    r3[xy] = s3[xy]

    ring2(0, 0)
    ring2(1, 0)

    @pl.loop(1, 16)
    def _(i):
        p3_from(i).wait_recv()

    @pl.loop(0, 8)
    def _(i):
        p4(i, 1 - g).start()

    @pl.loop(1, 8)
    def _(i):
        p4(i, g).start()

    r4[g, z, :, k] = r3[:, zk]

    for e in (-1, 1):
        for h in (0, 1):
            ring2(h, e)

    @pl.loop(1, 8)
    def _(i):
        p4_from(i, g).wait_recv()

    own.wait()
    here = r4[g].reshape(512, SPAN).T

    @pl.loop(0, 8)
    def _(t):
        cols = pl.ds(pl.multiple_of(t * TILE, TILE), TILE)
        acc[:, cols] = jnp.dot(here, wown[:, cols], preferred_element_type=f32)

    for h in (0, 1):
        ring2(h, 2)
    for e in (0, -1, 1):
        for h in (0, 1):
            ring2_far(h, e)

    @pl.loop(8, 16)
    def _(t):
        cols = pl.ds(pl.multiple_of(t * TILE, TILE), TILE)
        acc[:, cols] = jnp.dot(here, wown[:, cols], preferred_element_type=f32)

    for h in (0, 1):
        ring2_far(h, 2)

    @pl.loop(0, 8)
    def _(i):
        p4_from(i, 1 - g).wait_recv()

    there = r4[1 - g].reshape(512, SPAN).T

    @pl.loop(0, 16)
    def _(i):
        d2d(0, i, 1 - k).wait_recv()
        d2d(1, i, 1 - k).wait_recv()

    for part in range(4):
        for t in range(QUARTER // TILE):
            base = part * QUARTER + t * TILE
            weight = wo[part // 2, part % 2, :, :, t * TILE : (t + 1) * TILE].reshape(512, TILE)
            total = acc[:, base : base + TILE] + jnp.dot(there, weight, preferred_element_type=f32)
            out_ref[:, base : base + TILE] = total.astype(bf16)

    @pl.loop(1, 8)
    def _(i):
        p1(i, s1, r1, p1_s, p1_r).wait_send()
        p1(i, s1q, r1q, p1q_s, p1q_r).wait_send()
        p4(i, g).wait_send()

    @pl.loop(1, 16)
    def _(i):
        p2(i, r1, r2, p2_s, p2_r).wait_send()
        p2(i, r1q, r2q, p2q_s, p2q_r).wait_send()
        p3(i).wait_send()

    @pl.loop(0, 8)
    def _(i):
        p4(i, 1 - g).wait_send()

    @pl.loop(0, 16)
    def _(i):
        d2d(0, i, k).wait_send()
        d2d(1, i, k).wait_send()

    for h in (0, 1):
        for sub in (0, 1):
            seed(h, sub, False).wait_send()
            for side in (0, 1):
                st1(h, side, sub).wait_send()
                for e in (0, -1, 1, 2):
                    st2(h, e, side, sub).wait_send()
        st1(h, 0, 0, -1).wait_send()
        st1(h, 1, 1, 1).wait_send()
        for e in (0, -1, 1, 2):
            st2(h, e, 0, 0, -1).wait_send()
            st2(h, e, 1, 1, 1).wait_send()


def body(query_branch, key_branch, value_branch, filter_taps, skip_gain, out_weight):
    width = out_weight.shape[1]
    vmem, hbm = pl.BlockSpec(memory_space=pltpu.VMEM), pl.BlockSpec(memory_space=pl.ANY)
    dma = pltpu.SemaphoreType.DMA
    v = pltpu.VMEM
    return pl.pallas_call(
        kernel,
        out_shape=jax.ShapeDtypeStruct((SPAN, width), bf16),
        in_specs=[vmem] * 4 + [pl.BlockSpec(memory_space=pltpu.SMEM)] + [vmem] * 5 + [hbm],
        out_specs=vmem,
        scratch_shapes=[
            v((8, 16, 2 * CH, SPAN), bf16), v((8, 16, 2 * CH, SPAN), bf16), v((16, 8, 2 * CH, SPAN), bf16),
            v((8, 16, CH, SPAN), bf16), v((8, 16, CH, SPAN), bf16), v((16, 8, CH, SPAN), bf16),
            v((16, 8, CH, SPAN), bf16), v((16, 8, CH, SPAN), bf16), v((2, 4, 16, 2, CH, SPAN), bf16),
            v((512, width), bf16), v((2, 2, 32, 16, QUARTER), bf16), v((SPAN, width), f32),
            v((BLOCKS * 2 * CH, SPAN), f32), v((BLOCKS * CH, SPAN), f32),
            v((256, 2 * CH * SPAN), bf16), v((2 * CH * BLOCKS, 768), bf16), v((CH * BLOCKS, 768), bf16), v((768, CH * SPAN), bf16),
            dma, dma((8,)), dma((8,)), dma((8,)), dma((8,)), dma((16,)), dma((16,)), dma((16,)), dma((16,)),
            dma((16,)), dma((16,)), dma((2, 8)), dma((2, 8)),
            dma((2, 2)), dma((2, 2)), dma((2, 2, 2, 2)), dma((2, 2, 2, 2)), dma((2, 4, 2, 2, 2)), dma((2, 4, 2, 2, 2)),
            dma((2, 16)), dma((2, 16)),
        ],
        compiler_params=pltpu.CompilerParams(collective_id=0, has_side_effects=True, vmem_limit_bytes=56 * 2**20),
    )(query_branch, key_branch, value_branch, filter_taps, skip_gain.reshape(1, -1), *tables(), out_weight)


def solution(mesh):
    return jax.shard_map(
        body,
        mesh=mesh,
        in_specs=(P("seq", "ch"), P("seq", "ch"), P("seq", "ch"), P("seq", "ch"), P("ch"), P("ch", None)),
        out_specs=P("seq", None),
        check_vma=False,
    )
```

time: 258 us -> 73.7 us (0.29)
  waiting for transfers between devices: 162 us -> 0 us
  Pallas kernels: 0 us -> 70.5 us
  blocking collectives: 24.9 us -> 0 us
  starting transfers between devices: 19.1 us -> 0 us
  matrix products: 18.4 us -> 0 us
  local copies, waits for them, and re-layouts: 18.3 us -> 3.1 us
  between operations: 13.6 us -> 0.01 us
    all_gather x1 -> x0, waiting for transfers between devices: 149 us -> none  [body(): other_weight = lax.all_gather(theirs, 'seq', tiled=True)]
    pallas_call x0 -> x1, Pallas kernels: none -> 70.5 us  [body(): pl.pallas_call(kernel, out_shape=jax.ShapeDtypeStruct((SPAN, width), bf16...]
    all_to_all x1 -> x0, blocking collectives: 24.9 us -> none  [body(): got = lax.all_to_all(pair, 'seq', 0, 0)]
    dot_general x6 -> x0, matrix products: 18.4 us -> none  [the longest x1 7.3 us: body(): jnp.dot(gated_other, other_weight, preferred_element_type=f32)]
    unnamed x19 -> x1, local copies, waits for them, and re-layouts: 16.4 us -> 3.1 us
    ppermute x2 -> x0, starting transfers between devices: 12.6 us -> none  [the longest x1 7.83 us: body(): theirs = lax.ppermute(mine, 'ch', [(i, i ^ 1) for i in range(n_ch)])]
    all_to_all x1 -> x0, waiting for transfers between devices: 10.9 us -> none  [body(): conv = lax.all_to_all(y.astype(bf16), 'seq', 0, 0)]
    all_to_all x1 -> x0, starting transfers between devices: 6.44 us -> none  [body(): conv = lax.all_to_all(y.astype(bf16), 'seq', 0, 0)]
  transfers between devices with their start and end apart: 4 -> 0, of which waited for: 3 -> 0; matrix products, arithmetic and copies ran while one was open for 11% -> 0% of each run, Pallas kernels for 0% -> 0%
where the time goes in v2:
time: 73.7 us; the launch traced here: 73.6 us
  Pallas kernels  70.5 us (96%)
  local copies, waits for them, and re-layouts  3.1 us (4%)
    pallas_call x1, Pallas kernels, body(): pl.pallas_call(kernel, out_shape=jax.ShapeDtypeStruct((SPAN, width), bf16...  70.5 us
    unnamed x1, local copies, waits for them, and re-layouts  3.1 us

profile of v2, /device:TPU:1, one launch (start us, length us, event | category | flops | bytes accessed | tf_op | source)
XLA Modules:
  0.0 73.6 jit_solution(8342703752465052681)
XLA Ops:
  0.0 70.5 %shard_map.109 = bf16[128,8192]{1,0:T(8,128)(2,1)} custom-call(bf16[128,512]{1,0:T(8,128)(2,1)} %q_ref.1, bf16[128,512]{1,0:T(8,128)(2,1)} %k_ref.1, bf16[128,512]{1,0:T(8,128)(2,1)} %v_ref.1, f32[128,512]{1,0:T(8,128)} %taps_ref.1, f32[1,512]{1,0:T(1,128)} %bitcast.1, bf16[256,256]{1,0:T(8,128)(2,1)} %constant.10.clone.t1_ref, ...), custom_call_target="tpu_custom_call" | custom-call | tf_op jit(solution)/shard_map/pallas_call | solution.py:459
  70.5 3.1 %copy.13 = bf16[128,8192]{1,0:T(8,128)(2,1)} copy(bf16[128,8192]{1,0:T(8,128)(2,1)} %shard_map.109) | data formatting | bytes 4194304

commit v3 on v2

v3 whole, which is shorter than its diff:
```python
import functools
import math

import jax
import jax.numpy as jnp
import numpy as np
from jax import lax
from jax.experimental import pallas as pl
from jax.experimental.pallas import tpu as pltpu
from jax.sharding import PartitionSpec as P

bf16 = jnp.bfloat16
f32 = jnp.float32
MESH = pl.DeviceIdType.MESH
SPAN = 128
BLOCKS = 128
CH = 4
TILE = 512
QUARTER = 2048


def split(t):
    hi = t.astype(bf16)
    return hi, (t - hi.astype(f32)).astype(bf16)


def tables():
    n = 2 * BLOCKS
    at = np.arange(BLOCKS)
    a = (at % 8) // 2 * 32 + at // 8 * 2 + at % 2
    alpha = np.arange(BLOCKS)[:, None] + 0.5
    fine = np.arange(SPAN)
    ahead = 2.0 * np.pi * alpha * a[None, :] / n
    turn = 2.0 * np.pi * alpha * fine[None, :] / (n * SPAN)
    inner = 2.0 * np.pi * (fine[:, None] * fine[None, :] % SPAN) / SPAN
    first = np.concatenate([np.cos(ahead), -np.sin(ahead)], 0)
    second = np.block([[np.cos(inner), -np.sin(inner)], [np.sin(inner), np.cos(inner)]])
    back = np.block([[np.cos(inner), np.sin(inner)], [-np.sin(inner), np.cos(inner)]])
    last = first.T / (BLOCKS * SPAN)

    as32 = lambda t: jnp.asarray(t.astype(np.float32))
    return as32(first), as32(second), as32(back), as32(last), as32(np.stack([np.cos(turn), -np.sin(turn)]))


def kernel(
    q_hbm, k_hbm, v_hbm, taps_hbm, skip_ref, t1_hbm, t2_hbm, t3_hbm, t4_hbm, tw_hbm, w_ref, out_ref,
    q_ref, k_ref, v_ref, taps_ref, t1_raw, t2_raw, t3_raw, t4_raw, tw_ref, load_sem, t1_ref, t2_ref, t3_ref, t4_ref,
    s1, r1, r2, s1q, r1q, r2q, s3, r3, r4, wown, wo, acc, rows8, rows4, xcat, lhs2, lhs3, rhs4,
    own_sem, p1_s, p1_r, p1q_s, p1q_r, p2_s, p2_r, p2q_s, p2q_r, p3_s, p3_r, p4_s, p4_r,
    fresh_s, seed_r, st1_s, st1_r, st2_s, st2_r, d2d_s, d2d_r, result, out_sem,
):
    me = lax.axis_index("seq")
    g = lax.axis_index("ch")
    z, xy, k = me // 32, me // 2 % 16, me % 2
    x, y = xy // 4, xy % 4
    zk = z * 2 + k

    def dev(z_, xy_, k_, g_):
        return (z_ * 32 + xy_ * 2 + k_, g_)

    def remote(src, dst, ss, rs, to):
        return pltpu.make_async_remote_copy(
            src_ref=src, dst_ref=dst, send_sem=ss, recv_sem=rs, device_id=to, device_id_type=MESH
        )

    barrier = pltpu.get_barrier_semaphore()

    @pl.loop(1, 16)
    def _(i):
        pl.semaphore_signal(barrier, inc=1, device_id=dev(z, (xy + i) % 16, k, g), device_id_type=MESH)

    @pl.loop(1, 8)
    def _(i):
        to = (zk + i) % 8
        pl.semaphore_signal(barrier, inc=1, device_id=dev(to // 2, xy, to % 2, g), device_id_type=MESH)

    @pl.loop(0, 8)
    def _(i):
        pl.semaphore_signal(barrier, inc=1, device_id=dev(i // 2, xy, i % 2, 1 - g), device_id_type=MESH)

    loads = [
        pltpu.make_async_copy(src, dst, load_sem.at[i])
        for i, (src, dst) in enumerate([
            (k_hbm, k_ref), (v_hbm, v_ref), (taps_hbm, taps_ref), (q_hbm, q_ref),
            (t1_hbm, t1_raw), (t2_hbm, t2_raw), (t3_hbm, t3_raw), (t4_hbm, t4_raw), (tw_hbm, tw_ref),
        ])
    ]
    for load in loads:
        load.start()
    own = pltpu.make_async_copy(w_ref, wown, own_sem)
    own.start()
    for load in loads[:3]:
        load.wait()

    ut = (k_ref[...].astype(f32) * v_ref[...].astype(f32)).T
    ht = taps_ref[...].T
    both = jnp.concatenate([ut.reshape(BLOCKS, CH, SPAN), ht.reshape(BLOCKS, CH, SPAN)], 1).astype(bf16)
    both = both.reshape(4, 16, 2, 2 * CH, SPAN)
    for i in range(8):
        s1[i] = both[i // 2, :, i % 2]

    for load in loads[4:]:
        load.wait()
    hi, lo = split(t1_raw[...])
    t1_ref[:, 0:128] = hi
    t1_ref[:, 128:256] = lo
    for raw, ref in ((t2_raw, t2_ref), (t3_raw, t3_ref)):
        hi, lo = split(raw[...])
        ref[0:256, :] = hi
        ref[256:512, :] = hi
        ref[512:768, :] = lo
    hi, lo = split(t4_raw[...])
    t4_ref[:, 0:256] = hi
    t4_ref[:, 256:512] = hi
    t4_ref[:, 512:768] = lo

    pl.semaphore_wait(barrier, 30)

    def p1(i, src, dst, ss, rs):
        to = (zk + i) % 8
        return remote(src.at[to], dst.at[zk], ss.at[to], rs.at[zk], dev(to // 2, xy, to % 2, g))

    def p1_from(i, src, dst, ss, rs):
        fr = (zk + 8 - i) % 8
        return remote(src.at[fr], dst.at[fr], ss.at[fr], rs.at[fr], dev(fr // 2, xy, fr % 2, g))

    def p2(i, src, dst, ss, rs):
        to = (xy + i) % 16
        return remote(src.at[:, to], dst.at[xy], ss.at[to], rs.at[xy], dev(z, to, k, g))

    def p2_from(i, src, dst, ss, rs):
        fr = (xy + 16 - i) % 16
        return remote(src.at[:, fr], dst.at[fr], ss.at[fr], rs.at[fr], dev(z, fr, k, g))

    def p3(i):
        to = (xy + i) % 16
        return remote(s3.at[to], r3.at[xy], p3_s.at[to], p3_r.at[xy], dev(z, to, k, g))

    def p3_from(i):
        fr = (xy + 16 - i) % 16
        return remote(s3.at[fr], r3.at[fr], p3_s.at[fr], p3_r.at[fr], dev(z, fr, k, g))

    def p4(i, group):
        to = (zk + i) % 8
        return remote(
            r3.at[:, to], r4.at[g, z, :, k], p4_s.at[group, to], p4_r.at[g, zk], dev(to // 2, xy, to % 2, group)
        )

    def p4_from(i, group):
        fr = (zk + 8 - i) % 8
        return remote(
            r3.at[:, fr], r4.at[group, fr // 2, :, fr % 2], p4_s.at[group, fr], p4_r.at[group, fr],
            dev(fr // 2, xy, fr % 2, group),
        )

    def uv(h):
        return (x, y) if h == 0 else (y, x)

    def place(h, u, v):
        return u % 4 * 4 + v % 4 if h == 0 else v % 4 * 4 + u % 4

    def block(h, sub, at):
        return wo.at[h, sub, k * 16 + at]

    outer = (z + 1) % 4 < 2
    step = z // 2 * 2 - 1

    def fresh(h, sub, far):
        zn = (g * 4 + z + (1 + far) * step + 8) % 8
        src = w_ref.at[
            pl.ds(pl.multiple_of((k * 16 + xy) * 16, 16), 16), pl.ds((h * 2 + sub) * QUARTER, QUARTER)
        ]
        return remote(src, block(h, sub, xy), fresh_s.at[far, h, sub], seed_r.at[h, sub], dev(zn % 4, xy, k, zn // 4))

    def st1(h, side, sub):
        u, v = uv(h)
        to = place(h, u + 1 + side, v)
        return remote(
            block(h, sub, xy), block(h, sub, xy), st1_s.at[h, side, sub], st1_r.at[h, side, sub], dev(z, to, k, g)
        )

    def st2(h, e, side, sub, off=0):
        u, v = uv(h)
        at = place(h, u + e + 4, v + off + 4)
        slot = 0 if off == 0 else 1
        to = place(h, u, v + (1 if side == 0 else 3))
        return remote(
            block(h, sub, at), block(h, sub, at), st2_s.at[h, e % 4, slot, side, sub], st2_r.at[h, e % 4, slot, side, sub],
            dev(z, to, k, g),
        )

    def d2d(h, at, core):
        return remote(
            wo.at[h, :, core * 16 + at], wo.at[h, :, core * 16 + at], d2d_s.at[h, at], d2d_r.at[h, at], dev(z, xy, 1 - k, g)
        )

    def spread(h, e, sub):
        for side in (0, 1):
            st2(h, e, side, sub).start()

    def seed_step(h, sub):
        fresh(h, sub, 0).wait_recv()
        for side in (0, 1, 2):
            st1(h, side, sub).start()
        spread(h, 0, sub)
        if sub == 1:
            d2d(h, xy, k).start()

    def ring1(h, sub):
        u, v = uv(h)
        for side, e in ((0, -1), (2, 1), (1, 2)):
            st1(h, side, sub).wait_recv()
            spread(h, e, sub)
            if sub == 1:
                d2d(h, place(h, u + e + 4, v), k).start()

    def ring2(h, e):
        u, v = uv(h)
        for sub in (0, 1):
            st2(h, e, 0, sub).wait_recv()
            if sub == 0:
                st2(h, e, 0, 0, -1).start()
            st2(h, e, 1, sub).wait_recv()
            if sub == 1:
                st2(h, e, 1, 1, 1).start()
        d2d(h, place(h, u + e + 4, v + 3), k).start()
        d2d(h, place(h, u + e + 4, v + 1), k).start()

    def ring2_far(h, e):
        u, v = uv(h)
        st2(h, e, 0, 0, -1).wait_recv()
        st2(h, e, 1, 1, 1).wait_recv()
        d2d(h, place(h, u + e + 4, v + 2), k).start()

    def in1():
        @pl.loop(1, 8)
        def _(i):
            p1(i, s1, r1, p1_s, p1_r).start()

        r1[zk] = s1[zk]

    def in1q():
        loads[3].wait()
        qt = q_ref[...].astype(f32).T.reshape(BLOCKS, CH, SPAN).astype(bf16).reshape(4, 16, 2, CH, SPAN)
        for i in range(8):
            s1q[i] = qt[i // 2, :, i % 2]

        @pl.loop(1, 8)
        def _(i):
            p1(i, s1q, r1q, p1q_s, p1q_r).start()

        r1q[zk] = s1q[zk]

    def in2():
        @pl.loop(1, 8)
        def _(i):
            p1_from(i, s1, r1, p1_s, p1_r).wait_recv()

        @pl.loop(1, 16)
        def _(i):
            p2(i, r1, r2, p2_s, p2_r).start()

        r2[xy] = r1[:, xy]

    def in2q():
        @pl.loop(1, 8)
        def _(i):
            p1_from(i, s1q, r1q, p1q_s, p1q_r).wait_recv()

        @pl.loop(1, 16)
        def _(i):
            p2(i, r1q, r2q, p2q_s, p2q_r).start()

        r2q[xy] = r1q[:, xy]

    def forward():
        @pl.loop(1, 16)
        def _(i):
            p2_from(i, r1, r2, p2_s, p2_r).wait_recv()

        rows8[...] = r2[...].reshape(BLOCKS, 2 * CH, SPAN).astype(f32).reshape(BLOCKS * 2 * CH, SPAN)
        for r in range(2 * CH):
            part = rows8[pl.ds(r, BLOCKS, stride=2 * CH), :].astype(bf16)
            xcat[0:BLOCKS, r * SPAN : (r + 1) * SPAN] = part
            xcat[BLOCKS : 2 * BLOCKS, r * SPAN : (r + 1) * SPAN] = part
        for r in range(2 * CH):
            got = jnp.dot(t1_ref[...], xcat[:, r * SPAN : (r + 1) * SPAN], preferred_element_type=f32)
            re, im = got[:BLOCKS], got[BLOCKS:]
            hi, lo = split(jnp.concatenate([re * tw_ref[0] - im * tw_ref[1], re * tw_ref[1] + im * tw_ref[0]], 1))
            lhs2[r * BLOCKS : (r + 1) * BLOCKS, 0:256] = hi
            lhs2[r * BLOCKS : (r + 1) * BLOCKS, 256:512] = lo
            lhs2[r * BLOCKS : (r + 1) * BLOCKS, 512:768] = hi

    def middle():
        for c in range(CH):
            rows = pl.ds(c * BLOCKS, BLOCKS)
            left = jnp.dot(lhs2[rows, :], t2_ref[...], preferred_element_type=f32)
            right = jnp.dot(lhs2[pl.ds((c + CH) * BLOCKS, BLOCKS), :], t2_ref[...], preferred_element_type=f32)
            lr, li, rr, ri = left[:, :SPAN], left[:, SPAN:], right[:, :SPAN], right[:, SPAN:]
            hi, lo = split(jnp.concatenate([lr * rr - li * ri, lr * ri + li * rr], 1))
            lhs3[rows, 0:256] = hi
            lhs3[rows, 256:512] = lo
            lhs3[rows, 512:768] = hi
        for c in range(CH):
            rows = pl.ds(c * BLOCKS, BLOCKS)
            got = jnp.dot(lhs3[rows, :], t3_ref[...], preferred_element_type=f32)
            re, im = got[:, :SPAN], got[:, SPAN:]
            cols = pl.ds(c * SPAN, SPAN)
            hi, lo = split(jnp.concatenate([re * tw_ref[0] + im * tw_ref[1], im * tw_ref[0] - re * tw_ref[1]], 0))
            rhs4[0:256, cols] = hi
            rhs4[256:512, cols] = lo
            rhs4[512:768, cols] = hi

    def out1():
        @pl.loop(1, 16)
        def _(i):
            p2_from(i, r1q, r2q, p2q_s, p2q_r).wait_recv()

        rows4[...] = r2q[...].reshape(BLOCKS, CH, SPAN).astype(f32).reshape(BLOCKS * CH, SPAN)
        for c in range(CH):
            conv = jnp.dot(t4_ref[...], rhs4[:, c * SPAN : (c + 1) * SPAN], preferred_element_type=f32)
            at = pl.ds(c, BLOCKS, stride=CH)
            signal = rows8[pl.ds(c, BLOCKS, stride=2 * CH), :]
            rows4[at, :] = rows4[at, :] * (conv + skip_ref[0, me * CH + c] * signal)
        s3[...] = rows4[...].astype(bf16).reshape(16, 8, CH, SPAN)

        @pl.loop(1, 16)
        def _(i):
            p3(i).start()

        r3[xy] = s3[xy]

    def out2():
        @pl.loop(1, 16)
        def _(i):
            p3_from(i).wait_recv()

        @pl.loop(1, 8)
        def _(i):
            p4(i, g).start()

        @pl.loop(0, 8)
        def _(i):
            p4(i, 1 - g).start()

        r4[g, z, :, k] = r3[:, zk]

    def project_here():
        @pl.loop(1, 8)
        def _(i):
            p4_from(i, g).wait_recv()

        own.wait()
        here = r4[g].reshape(512, SPAN).T

        @pl.loop(0, 16)
        def _(t):
            cols = pl.ds(pl.multiple_of(t * TILE, TILE), TILE)
            acc[:, cols] = jnp.dot(here, wown[:, cols], preferred_element_type=f32)

    def leave(part, t):
        cols = pl.ds(part * QUARTER + t * TILE, TILE)
        return pltpu.make_async_copy(result.at[:, cols], out_ref.at[:, cols], out_sem.at[part, t])

    def project_there():
        @pl.loop(0, 8)
        def _(i):
            p4_from(i, 1 - g).wait_recv()

        there = r4[1 - g].reshape(512, SPAN).T
        for part in range(4):
            if part % 2 == 0:

                @pl.loop(0, 16)
                def _(i):
                    d2d(part // 2, i, 1 - k).wait_recv()

            for t in range(QUARTER // TILE):
                base = part * QUARTER + t * TILE
                weight = wo[part // 2, part % 2, :, :, t * TILE : (t + 1) * TILE].reshape(512, TILE)
                total = acc[:, base : base + TILE] + jnp.dot(there, weight, preferred_element_type=f32)
                result[:, base : base + TILE] = total.astype(bf16)
                leave(part, t).start()


    @pl.when(outer)
    def _():
        for sub in (0, 1):
            for h in (0, 1):
                for far in (0, 1):
                    fresh(h, sub, far).start()

    in1()
    in1q()
    seed_step(0, 0)
    seed_step(1, 0)
    in2()
    seed_step(0, 1)
    in2q()
    ring1(0, 0)
    seed_step(1, 1)
    ring1(1, 0)
    forward()
    ring1(0, 1)
    middle()
    out1()
    ring1(1, 1)
    ring2(0, 0)
    ring2(1, 0)
    out2()
    for e in (-1, 1, 2):
        for h in (0, 1):
            ring2(h, e)
    project_here()
    for e in (0, -1, 1, 2):
        for h in (0, 1):
            ring2_far(h, e)
    project_there()

    @pl.loop(1, 8)
    def _(i):
        p1(i, s1, r1, p1_s, p1_r).wait_send()
        p1(i, s1q, r1q, p1q_s, p1q_r).wait_send()
        p4(i, g).wait_send()

    @pl.loop(1, 16)
    def _(i):
        p2(i, r1, r2, p2_s, p2_r).wait_send()
        p2(i, r1q, r2q, p2q_s, p2q_r).wait_send()
        p3(i).wait_send()

    @pl.loop(0, 8)
    def _(i):
        p4(i, 1 - g).wait_send()

    @pl.loop(0, 16)
    def _(i):
        d2d(0, i, k).wait_send()
        d2d(1, i, k).wait_send()

    @pl.when(outer)
    def _():
        for h in (0, 1):
            for sub in (0, 1):
                for far in (0, 1):
                    fresh(h, sub, far).wait_send()

    for h in (0, 1):
        for sub in (0, 1):
            for side in (0, 1, 2):
                st1(h, side, sub).wait_send()
            for side in (0, 1):
                for e in (0, -1, 1, 2):
                    st2(h, e, side, sub).wait_send()
        for e in (0, -1, 1, 2):
            st2(h, e, 0, 0, -1).wait_send()
            st2(h, e, 1, 1, 1).wait_send()
    for part in range(4):
        for t in range(QUARTER // TILE):
            leave(part, t).wait()


def body(query_branch, key_branch, value_branch, filter_taps, skip_gain, out_weight):
    width = out_weight.shape[1]
    hbm = pl.BlockSpec(memory_space=pltpu.HBM)
    dma = pltpu.SemaphoreType.DMA
    v = pltpu.VMEM
    consts = tables()
    return pl.pallas_call(
        kernel,
        out_shape=jax.ShapeDtypeStruct((SPAN, width), bf16),
        in_specs=[hbm] * 4 + [pl.BlockSpec(memory_space=pltpu.SMEM)] + [hbm] * 6,
        out_specs=hbm,
        scratch_shapes=[
            v((SPAN, 512), bf16), v((SPAN, 512), bf16), v((SPAN, 512), bf16), v((SPAN, 512), f32),
            *[v(t.shape, t.dtype) for t in consts], dma((9,)),
            v((256, 256), bf16), v((768, 256), bf16), v((768, 256), bf16), v((128, 768), bf16),
            v((8, 16, 2 * CH, SPAN), bf16), v((8, 16, 2 * CH, SPAN), bf16), v((16, 8, 2 * CH, SPAN), bf16),
            v((8, 16, CH, SPAN), bf16), v((8, 16, CH, SPAN), bf16), v((16, 8, CH, SPAN), bf16),
            v((16, 8, CH, SPAN), bf16), v((16, 8, CH, SPAN), bf16), v((2, 4, 16, 2, CH, SPAN), bf16),
            v((512, width), bf16), v((2, 2, 32, 16, QUARTER), bf16), v((SPAN, width), f32),
            v((BLOCKS * 2 * CH, SPAN), f32), v((BLOCKS * CH, SPAN), f32),
            v((256, 2 * CH * SPAN), bf16), v((2 * CH * BLOCKS, 768), bf16), v((CH * BLOCKS, 768), bf16), v((768, CH * SPAN), bf16),
            dma, dma((8,)), dma((8,)), dma((8,)), dma((8,)), dma((16,)), dma((16,)), dma((16,)), dma((16,)),
            dma((16,)), dma((16,)), dma((2, 8)), dma((2, 8)),
            dma((2, 2, 2)), dma((2, 2)), dma((2, 3, 2)), dma((2, 3, 2)), dma((2, 4, 2, 2, 2)), dma((2, 4, 2, 2, 2)),
            dma((2, 16)), dma((2, 16)), v((SPAN, width), bf16), dma((4, QUARTER // TILE)),
        ],
        compiler_params=pltpu.CompilerParams(collective_id=0, has_side_effects=True, vmem_limit_bytes=56 * 2**20),
    )(query_branch, key_branch, value_branch, filter_taps, skip_gain.reshape(1, -1), *consts, out_weight)
def solution(mesh):
    return jax.shard_map(
        body,
        mesh=mesh,
        in_specs=(P("seq", "ch"), P("seq", "ch"), P("seq", "ch"), P("seq", "ch"), P("ch"), P("ch", None)),
        out_specs=P("seq", None),
        check_vma=False,
    )
```

time: 73.7 us -> 64.2 us (0.87)
  Pallas kernels: 70.5 us -> 60.9 us
    pallas_call x1, Pallas kernels: 70.5 us -> 60.9 us  [body(): pl.pallas_call(kernel, out_shape=jax.ShapeDtypeStruct((SPAN, width), bf16...]
where the time goes in v3:
time: 64.2 us; the launch traced here: 64 us
  Pallas kernels  60.9 us (95%)
  local copies, waits for them, and re-layouts  3.1 us (5%)
    pallas_call x1, Pallas kernels, body(): pl.pallas_call(kernel, out_shape=jax.ShapeDtypeStruct((SPAN, width), bf16...  60.9 us
    unnamed x1, local copies, waits for them, and re-layouts  3.1 us

profile of v3, /device:TPU:1, one launch (start us, length us, event | category | flops | bytes accessed | tf_op | source)
XLA Modules:
  0.0 64.0 jit_solution(6514103532523412251)
XLA Ops:
  0.0 60.9 %shard_map.109 = bf16[128,8192]{1,0:T(8,128)(2,1)} custom-call(bf16[128,512]{1,0:T(8,128)(2,1)} %q_hbm.1, bf16[128,512]{1,0:T(8,128)(2,1)} %k_hbm.1, bf16[128,512]{1,0:T(8,128)(2,1)} %v_hbm.1, f32[128,512]{1,0:T(8,128)} %taps_hbm.1, f32[1,512]{1,0:T(1,128)} %bitcast.1, f32[256,128]{1,0:T(8,128)} %constant.10.clone.t1_hbm, f32[256,256]{1,0:T(8,128)} %constant.11.clone.t2_hbm, ...), custom_call_target="tpu_custom_call" | custom-call | tf_op jit(solution)/shard_map/pallas_call | solution.py:469
  60.9 3.1 %copy.13 = bf16[128,8192]{1,0:T(8,128)(2,1)} copy(bf16[128,8192]{1,0:T(8,128)(2,1)} %shard_map.109) | data formatting | bytes 4194304

commit v4 on v3

--- a/solution.py
+++ b/solution.py
@@ -47,7 +47,7 @@
     q_ref, k_ref, v_ref, taps_ref, t1_raw, t2_raw, t3_raw, t4_raw, tw_ref, load_sem, t1_ref, t2_ref, t3_ref, t4_ref,
     s1, r1, r2, s1q, r1q, r2q, s3, r3, r4, wown, wo, acc, rows8, rows4, xcat, lhs2, lhs3, rhs4,
     own_sem, p1_s, p1_r, p1q_s, p1q_r, p2_s, p2_r, p2q_s, p2q_r, p3_s, p3_r, p4_s, p4_r,
-    fresh_s, seed_r, st1_s, st1_r, st2_s, st2_r, d2d_s, d2d_r, result, out_sem,
+    ring_s, fresh_s, seed_r, st1_r, st2_r, far_r, d2d_s, d2d_r, result, out_sem,
 ):
     me = lax.axis_index("seq")
     g = lax.axis_index("ch")
@@ -118,40 +118,22 @@
 
     def p1(i, src, dst, ss, rs):
         to = (zk + i) % 8
-        return remote(src.at[to], dst.at[zk], ss.at[to], rs.at[zk], dev(to // 2, xy, to % 2, g))
-
-    def p1_from(i, src, dst, ss, rs):
-        fr = (zk + 8 - i) % 8
-        return remote(src.at[fr], dst.at[fr], ss.at[fr], rs.at[fr], dev(fr // 2, xy, fr % 2, g))
+        return remote(src.at[to], dst.at[zk], ss, rs, dev(to // 2, xy, to % 2, g))
 
     def p2(i, src, dst, ss, rs):
         to = (xy + i) % 16
-        return remote(src.at[:, to], dst.at[xy], ss.at[to], rs.at[xy], dev(z, to, k, g))
-
-    def p2_from(i, src, dst, ss, rs):
-        fr = (xy + 16 - i) % 16
-        return remote(src.at[:, fr], dst.at[fr], ss.at[fr], rs.at[fr], dev(z, fr, k, g))
+        return remote(src.at[:, to], dst.at[xy], ss, rs, dev(z, to, k, g))
 
     def p3(i):
         to = (xy + i) % 16
-        return remote(s3.at[to], r3.at[xy], p3_s.at[to], p3_r.at[xy], dev(z, to, k, g))
-
-    def p3_from(i):
-        fr = (xy + 16 - i) % 16
-        return remote(s3.at[fr], r3.at[fr], p3_s.at[fr], p3_r.at[fr], dev(z, fr, k, g))
+        return remote(s3.at[to], r3.at[xy], p3_s, p3_r, dev(z, to, k, g))
 
     def p4(i, group):
         to = (zk + i) % 8
-        return remote(
-            r3.at[:, to], r4.at[g, z, :, k], p4_s.at[group, to], p4_r.at[g, zk], dev(to // 2, xy, to % 2, group)
-        )
-
-    def p4_from(i, group):
-        fr = (zk + 8 - i) % 8
-        return remote(
-            r3.at[:, fr], r4.at[group, fr // 2, :, fr % 2], p4_s.at[group, fr], p4_r.at[group, fr],
-            dev(fr // 2, xy, fr % 2, group),
-        )
+        return remote(r3.at[:, to], r4.at[g, z, :, k], p4_s.at[group], p4_r.at[g], dev(to // 2, xy, to % 2, group))
+
+    def all_of(ref, ss, rs):
+        return remote(ref, ref, ss, rs, dev(z, xy, 1 - k, g))
 
     def uv(h):
         return (x, y) if h == 0 else (y, x)
@@ -165,72 +147,67 @@
     outer = (z + 1) % 4 < 2
     step = z // 2 * 2 - 1
 
+    zn, zf = (g * 4 + z + step + 8) % 8, (g * 4 + z + 2 * step + 8) % 8
+    beyond = (dev(zn % 4, xy, k, zn // 4), dev(zf % 4, xy, k, zf // 4))
+
     def fresh(h, sub, far):
-        zn = (g * 4 + z + (1 + far) * step + 8) % 8
         src = w_ref.at[
             pl.ds(pl.multiple_of((k * 16 + xy) * 16, 16), 16), pl.ds((h * 2 + sub) * QUARTER, QUARTER)
         ]
-        return remote(src, block(h, sub, xy), fresh_s.at[far, h, sub], seed_r.at[h, sub], dev(zn % 4, xy, k, zn // 4))
+        return remote(src, block(h, sub, xy), fresh_s, seed_r.at[h, sub], beyond[far])
 
     def st1(h, side, sub):
         u, v = uv(h)
         to = place(h, u + 1 + side, v)
-        return remote(
-            block(h, sub, xy), block(h, sub, xy), st1_s.at[h, side, sub], st1_r.at[h, side, sub], dev(z, to, k, g)
-        )
-
-    def st2(h, e, side, sub, off=0):
-        u, v = uv(h)
-        at = place(h, u + e + 4, v + off + 4)
-        slot = 0 if off == 0 else 1
+        return remote(block(h, sub, xy), block(h, sub, xy), ring_s, st1_r.at[h], dev(z, to, k, g))
+
+    def st2(h, e, side):
+        u, v = uv(h)
+        there = wo.at[h, :, k * 16 + place(h, u + e + 4, v)]
         to = place(h, u, v + (1 if side == 0 else 3))
-        return remote(
-            block(h, sub, at), block(h, sub, at), st2_s.at[h, e % 4, slot, side, sub], st2_r.at[h, e % 4, slot, side, sub],
-            dev(z, to, k, g),
-        )
-
-    def d2d(h, at, core):
-        return remote(
-            wo.at[h, :, core * 16 + at], wo.at[h, :, core * 16 + at], d2d_s.at[h, at], d2d_r.at[h, at], dev(z, xy, 1 - k, g)
-        )
-
-    def spread(h, e, sub):
+        return remote(there, there, ring_s, st2_r.at[h, e % 4], dev(z, to, k, g))
+
+    def st2_on(h, e, side):
+        u, v = uv(h)
+        there = block(h, side, place(h, u + e + 4, v + (3 if side == 0 else 1)))
+        to = place(h, u, v + (1 if side == 0 else 3))
+        return remote(there, there, ring_s, far_r.at[h, e % 4], dev(z, to, k, g))
+
+    def d2d(h, at):
+        there = wo.at[h, :, k * 16 + at]
+        return remote(there, there, d2d_s, d2d_r.at[h], dev(z, xy, 1 - k, g))
+
+    def spread(h, e):
         for side in (0, 1):
-            st2(h, e, side, sub).start()
+            st2(h, e, side).start()
 
     def seed_step(h, sub):
-        fresh(h, sub, 0).wait_recv()
+        all_of(wo.at[0, 0, 0], fresh_s, seed_r.at[h, sub]).wait_recv()
         for side in (0, 1, 2):
             st1(h, side, sub).start()
-        spread(h, 0, sub)
         if sub == 1:
-            d2d(h, xy, k).start()
-
-    def ring1(h, sub):
-        u, v = uv(h)
-        for side, e in ((0, -1), (2, 1), (1, 2)):
-            st1(h, side, sub).wait_recv()
-            spread(h, e, sub)
-            if sub == 1:
-                d2d(h, place(h, u + e + 4, v), k).start()
+            d2d(h, xy).start()
+
+    def ring1(h):
+        u, v = uv(h)
+        all_of(wo.at[0, 0, 0:6], ring_s, st1_r.at[h]).wait_recv()
+        for e in (-1, 1, 2):
+            spread(h, e)
+        for e in (-1, 1, 2):
+            d2d(h, place(h, u + e + 4, v)).start()
 
     def ring2(h, e):
         u, v = uv(h)
-        for sub in (0, 1):
-            st2(h, e, 0, sub).wait_recv()
-            if sub == 0:
-                st2(h, e, 0, 0, -1).start()
-            st2(h, e, 1, sub).wait_recv()
-            if sub == 1:
-                st2(h, e, 1, 1, 1).start()
-        d2d(h, place(h, u + e + 4, v + 3), k).start()
-        d2d(h, place(h, u + e + 4, v + 1), k).start()
+        all_of(wo.at[0, 0, 0:4], ring_s, st2_r.at[h, e % 4]).wait_recv()
+        for side in (0, 1):
+            st2_on(h, e, side).start()
+        for off in (1, 3):
+            d2d(h, place(h, u + e + 4, v + off)).start()
 
     def ring2_far(h, e):
         u, v = uv(h)
-        st2(h, e, 0, 0, -1).wait_recv()
-        st2(h, e, 1, 1, 1).wait_recv()
-        d2d(h, place(h, u + e + 4, v + 2), k).start()
+        all_of(wo.at[0, 0, 0:2], ring_s, far_r.at[h, e % 4]).wait_recv()
+        d2d(h, place(h, u + e + 4, v + 2)).start()
 
     def in1():
         @pl.loop(1, 8)
@@ -245,6 +222,7 @@
         for i in range(8):
             s1q[i] = qt[i // 2, :, i % 2]
 
+    def in1q_send():
         @pl.loop(1, 8)
         def _(i):
             p1(i, s1q, r1q, p1q_s, p1q_r).start()
@@ -252,9 +230,7 @@
         r1q[zk] = s1q[zk]
 
     def in2():
-        @pl.loop(1, 8)
-        def _(i):
-            p1_from(i, s1, r1, p1_s, p1_r).wait_recv()
+        all_of(r1.at[0:7], p1_s, p1_r).wait_recv()
 
         @pl.loop(1, 16)
         def _(i):
@@ -263,9 +239,7 @@
         r2[xy] = r1[:, xy]
 
     def in2q():
-        @pl.loop(1, 8)
-        def _(i):
-            p1_from(i, s1q, r1q, p1q_s, p1q_r).wait_recv()
+        all_of(r1q.at[0:7], p1q_s, p1q_r).wait_recv()
 
         @pl.loop(1, 16)
         def _(i):
@@ -274,9 +248,7 @@
         r2q[xy] = r1q[:, xy]
 
     def forward():
-        @pl.loop(1, 16)
-        def _(i):
-            p2_from(i, r1, r2, p2_s, p2_r).wait_recv()
+        all_of(r2.at[0:15], p2_s, p2_r).wait_recv()
 
         rows8[...] = r2[...].reshape(BLOCKS, 2 * CH, SPAN).astype(f32).reshape(BLOCKS * 2 * CH, SPAN)
         for r in range(2 * CH):
@@ -312,9 +284,7 @@
             rhs4[512:768, cols] = hi
 
     def out1():
-        @pl.loop(1, 16)
-        def _(i):
-            p2_from(i, r1q, r2q, p2q_s, p2q_r).wait_recv()
+        all_of(r2q.at[0:15], p2q_s, p2q_r).wait_recv()
 
         rows4[...] = r2q[...].reshape(BLOCKS, CH, SPAN).astype(f32).reshape(BLOCKS * CH, SPAN)
         for c in range(CH):
@@ -331,9 +301,7 @@
         r3[xy] = s3[xy]
 
     def out2():
-        @pl.loop(1, 16)
-        def _(i):
-            p3_from(i).wait_recv()
+        all_of(r3.at[0:15], p3_s, p3_r).wait_recv()
 
         @pl.loop(1, 8)
         def _(i):
@@ -346,9 +314,7 @@
         r4[g, z, :, k] = r3[:, zk]
 
     def project_here():
-        @pl.loop(1, 8)
-        def _(i):
-            p4_from(i, g).wait_recv()
+        all_of(r3.at[0:14], p4_s.at[g], p4_r.at[g]).wait_recv()
 
         own.wait()
         here = r4[g].reshape(512, SPAN).T
@@ -358,29 +324,41 @@
             cols = pl.ds(pl.multiple_of(t * TILE, TILE), TILE)
             acc[:, cols] = jnp.dot(here, wown[:, cols], preferred_element_type=f32)
 
-    def leave(part, t):
-        cols = pl.ds(part * QUARTER + t * TILE, TILE)
-        return pltpu.make_async_copy(result.at[:, cols], out_ref.at[:, cols], out_sem.at[part, t])
+    def leave(i, base, size):
+        cols = pl.ds(base, size)
+        return pltpu.make_async_copy(result.at[:, cols], out_ref.at[:, cols], out_sem.at[i])
+
+    leaving = [(t * TILE, TILE) for t in range(16)]
 
     def project_there():
-        @pl.loop(0, 8)
-        def _(i):
-            p4_from(i, 1 - g).wait_recv()
+        all_of(r3, p4_s.at[1 - g], p4_r.at[1 - g]).wait_recv()
 
         there = r4[1 - g].reshape(512, SPAN).T
+
+        def finish(i, weight):
+            base, size = leaving[i]
+            total = acc[:, base : base + size] + jnp.dot(there, weight.reshape(512, size), preferred_element_type=f32)
+            result[:, base : base + size] = total.astype(bf16)
+            leave(i, base, size).start()
+
         for part in range(4):
             if part % 2 == 0:
 
-                @pl.loop(0, 16)
-                def _(i):
-                    d2d(part // 2, i, 1 - k).wait_recv()
-
-            for t in range(QUARTER // TILE):
-                base = part * QUARTER + t * TILE
-                weight = wo[part // 2, part % 2, :, :, t * TILE : (t + 1) * TILE].reshape(512, TILE)
-                total = acc[:, base : base + TILE] + jnp.dot(there, weight, preferred_element_type=f32)
-                result[:, base : base + TILE] = total.astype(bf16)
-                leave(part, t).start()
+                all_of(wo.at[0, :, 0:16], d2d_s, d2d_r.at[part // 2]).wait_recv()
+
+            for t in range(4):
+                finish(part * 4 + t, wo[part // 2, part % 2, :, :, t * TILE : (t + 1) * TILE])
+
+    def sent():
+        all_of(s1.at[0:7], p1_s, p1_r).wait_send()
+        all_of(s1q.at[0:7], p1q_s, p1q_r).wait_send()
+        all_of(r2.at[0:15], p2_s, p2_r).wait_send()
+        all_of(r2q.at[0:15], p2q_s, p2q_r).wait_send()
+        all_of(s3.at[0:15], p3_s, p3_r).wait_send()
+
+        @pl.when(outer)
+        def _():
+            all_of(wo.at[0, 0, 0:8], fresh_s, seed_r.at[0, 0]).wait_send()
 
 
     @pl.when(outer)
@@ -392,72 +370,37 @@
 
     in1()
     in1q()
+    in1q_send()
     seed_step(0, 0)
     seed_step(1, 0)
     in2()
     seed_step(0, 1)
     in2q()
-    ring1(0, 0)
     seed_step(1, 1)
-    ring1(1, 0)
     forward()
-    ring1(0, 1)
+    spread(0, 0)
+    spread(1, 0)
     middle()
     out1()
-    ring1(1, 1)
-    ring2(0, 0)
-    ring2(1, 0)
+    ring1(0)
+    ring1(1)
     out2()
-    for e in (-1, 1, 2):
+    for e in (0, -1, 1, 2):
         for h in (0, 1):
             ring2(h, e)
     project_here()
+    sent()
     for e in (0, -1, 1, 2):
         for h in (0, 1):
             ring2_far(h, e)
     project_there()
 
-    @pl.loop(1, 8)
-    def _(i):
-        p1(i, s1, r1, p1_s, p1_r).wait_send()
-        p1(i, s1q, r1q, p1q_s, p1q_r).wait_send()
-        p4(i, g).wait_send()
-
-    @pl.loop(1, 16)
-    def _(i):
-        p2(i, r1, r2, p2_s, p2_r).wait_send()
-        p2(i, r1q, r2q, p2q_s, p2q_r).wait_send()
-        p3(i).wait_send()
-
-    @pl.loop(0, 8)
-    def _(i):
-        p4(i, 1 - g).wait_send()
-
-    @pl.loop(0, 16)
-    def _(i):
-        d2d(0, i, k).wait_send()
-        d2d(1, i, k).wait_send()
-
-    @pl.when(outer)
-    def _():
-        for h in (0, 1):
-            for sub in (0, 1):
-                for far in (0, 1):
-                    fresh(h, sub, far).wait_send()
-
-    for h in (0, 1):
-        for sub in (0, 1):
-            for side in (0, 1, 2):
-                st1(h, side, sub).wait_send()
-            for side in (0, 1):
-                for e in (0, -1, 1, 2):
-                    st2(h, e, side, sub).wait_send()
-        for e in (0, -1, 1, 2):
-            st2(h, e, 0, 0, -1).wait_send()
-            st2(h, e, 1, 1, 1).wait_send()
-    for part in range(4):
-        for t in range(QUARTER // TILE):
-            leave(part, t).wait()
+    all_of(r3.at[0:14], p4_s.at[g], p4_r.at[g]).wait_send()
+    all_of(r3, p4_s.at[1 - g], p4_r.at[1 - g]).wait_send()
+    all_of(wo.at[:, :, 0:16], d2d_s, d2d_r.at[0]).wait_send()
+    all_of(wo.at[:, :, 0:15], ring_s, st1_r.at[0]).wait_send()
+    for i, (base, size) in enumerate(leaving):
+        leave(i, base, size).wait()
 
 
 def body(query_branch, key_branch, value_branch, filter_taps, skip_gain, out_weight):
@@ -481,10 +424,8 @@
             v((512, width), bf16), v((2, 2, 32, 16, QUARTER), bf16), v((SPAN, width), f32),
             v((BLOCKS * 2 * CH, SPAN), f32), v((BLOCKS * CH, SPAN), f32),
             v((256, 2 * CH * SPAN), bf16), v((2 * CH * BLOCKS, 768), bf16), v((CH * BLOCKS, 768), bf16), v((768, CH * SPAN), bf16),
-            dma, dma((8,)), dma((8,)), dma((8,)), dma((8,)), dma((16,)), dma((16,)), dma((16,)), dma((16,)),
-            dma((16,)), dma((16,)), dma((2, 8)), dma((2, 8)),
-            dma((2, 2, 2)), dma((2, 2)), dma((2, 3, 2)), dma((2, 3, 2)), dma((2, 4, 2, 2, 2)), dma((2, 4, 2, 2, 2)),
-            dma((2, 16)), dma((2, 16)), v((SPAN, width), bf16), dma((4, QUARTER // TILE)),
+            dma, dma, dma, dma, dma, dma, dma, dma, dma, dma, dma, dma((2,)), dma((2,)),
+            dma, dma, dma((2, 2)), dma((2,)), dma((2, 4)), dma((2, 4)), dma, dma((2,)), v((SPAN, width), bf16), dma((16,)),
         ],
         compiler_params=pltpu.CompilerParams(collective_id=0, has_side_effects=True, vmem_limit_bytes=56 * 2**20),
     )(query_branch, key_branch, value_branch, filter_taps, skip_gain.reshape(1, -1), *consts, out_weight)

time: 64.2 us -> 55.6 us (0.87)
  Pallas kernels: 60.9 us -> 52.3 us
    pallas_call x1, Pallas kernels: 60.9 us -> 52.3 us  [body(): pl.pallas_call(kernel, out_shape=jax.ShapeDtypeStruct((SPAN, width), bf16...]
where the time goes in v4:
time: 55.6 us; the launch traced here: 55.4 us
  Pallas kernels  52.3 us (94%)
  local copies, waits for them, and re-layouts  3.1 us (6%)
    pallas_call x1, Pallas kernels, body(): pl.pallas_call(kernel, out_shape=jax.ShapeDtypeStruct((SPAN, width), bf16...  52.3 us
    unnamed x1, local copies, waits for them, and re-layouts  3.1 us

profile of v4, /device:TPU:1, one launch (start us, length us, event | category | flops | bytes accessed | tf_op | source)
XLA Modules:
  0.0 55.4 jit_solution(13318490372429611024)
XLA Ops:
  0.0 52.3 %shard_map.109 = bf16[128,8192]{1,0:T(8,128)(2,1)} custom-call(bf16[128,512]{1,0:T(8,128)(2,1)} %q_hbm.1, bf16[128,512]{1,0:T(8,128)(2,1)} %k_hbm.1, bf16[128,512]{1,0:T(8,128)(2,1)} %v_hbm.1, f32[128,512]{1,0:T(8,128)} %taps_hbm.1, f32[1,512]{1,0:T(1,128)} %bitcast.1, f32[256,128]{1,0:T(8,128)} %constant.10.clone.t1_hbm, f32[256,256]{1,0:T(8,128)} %constant.11.clone.t2_hbm, ...), custom_call_target="tpu_custom_call" | custom-call | tf_op jit(solution)/shard_map/pallas_call | solution.py:412
  52.3 3.1 %copy.13 = bf16[128,8192]{1,0:T(8,128)(2,1)} copy(bf16[128,8192]{1,0:T(8,128)(2,1)} %shard_map.109) | data formatting | bytes 4194304

commit v5 on v4

--- a/solution.py
+++ b/solution.py
@@ -117,7 +117,7 @@
     pl.semaphore_wait(barrier, 30)
 
     def p1(i, src, dst, ss, rs):
-        to = (zk + i) % 8
+        to = (zk + (z // 2 * 2 - 1) * i + 8) % 8
         return remote(src.at[to], dst.at[zk], ss, rs, dev(to // 2, xy, to % 2, g))
 
     def p2(i, src, dst, ss, rs):

time: 55.6 us -> 56.3 us (1.013); the launches traced: 55.4 us -> 55.4 us
  no operation moved by 1% of the time
where the time goes in v5:
time: 56.3 us; the launch traced here: 55.4 us
  Pallas kernels  52.3 us (93%)
  local copies, waits for them, and re-layouts  3.1 us (6%)
    pallas_call x1, Pallas kernels, body(): pl.pallas_call(kernel, out_shape=jax.ShapeDtypeStruct((SPAN, width), bf16...  52.3 us
    unnamed x1, local copies, waits for them, and re-layouts  3.1 us

profile of v5, /device:TPU:1, one launch (start us, length us, event | category | flops | bytes accessed | tf_op | source)
XLA Modules:
  0.0 55.4 jit_solution(14378561603620565279)
XLA Ops:
  0.0 52.3 %shard_map.109 = bf16[128,8192]{1,0:T(8,128)(2,1)} custom-call(bf16[128,512]{1,0:T(8,128)(2,1)} %q_hbm.1, bf16[128,512]{1,0:T(8,128)(2,1)} %k_hbm.1, bf16[128,512]{1,0:T(8,128)(2,1)} %v_hbm.1, f32[128,512]{1,0:T(8,128)} %taps_hbm.1, f32[1,512]{1,0:T(1,128)} %bitcast.1, f32[256,128]{1,0:T(8,128)} %constant.10.clone.t1_hbm, f32[256,256]{1,0:T(8,128)} %constant.11.clone.t2_hbm, ...), custom_call_target="tpu_custom_call" | custom-call | tf_op jit(solution)/shard_map/pallas_call | solution.py:412
  52.3 3.1 %copy.13 = bf16[128,8192]{1,0:T(8,128)(2,1)} copy(bf16[128,8192]{1,0:T(8,128)(2,1)} %shard_map.109) | data formatting | bytes 4194304
